TPU v7x, 512 devices: a whole 4x4x16 slice. The times are simulated.
512 devices in a mesh: ctx: 64 (over x, z), tp: 8 (over y, core).
Axes of the slice: x: 4, y: 4, z: 16, core: 2. Of those that a mesh axis runs over, the one named last changes fastest.
Arguments:
- query_in: bfloat16 [16384, 4096], P('ctx', 'tp'), may hold values from -6 to 6
- key_in: bfloat16 [16384, 4096], P('ctx', 'tp'), may hold values from -6 to 6
- value_in: bfloat16 [16384, 4096], P('ctx', 'tp'), may hold values from -6 to 6
- short_weights: float32 [3, 3, 4096], P(None, None, 'tp'), may hold values from -3 to 3
- long_filter: float32 [4096, 16384], P(('tp', 'ctx')), may hold values from -1.6 to 1.6
- skip_gain: float32 [4096], P(('tp', 'ctx')), may hold values from -4 to 4
- cotangent: bfloat16 [16384, 4096], P('ctx', 'tp'), may hold values from -10.8 to 10.8
Outputs:
- mixed_out: bfloat16 [16384, 4096], P('ctx', 'tp')
- d_query: bfloat16 [16384, 4096], P('ctx', 'tp')
- d_key: bfloat16 [16384, 4096], P('ctx', 'tp')
- d_value: bfloat16 [16384, 4096], P('ctx', 'tp')
- d_filter: float32 [4096, 16384], P(('tp', 'ctx'))
- d_skip: float32 [4096], P(('tp', 'ctx'))
- d_short: float32 [3, 3, 4096], P(None, None, 'tp')
All inputs are finite; a program needn't handle non-finite values.
Results may differ from a plain program's by a relative error of at most 0.0064.
Values may be sent and summed in bfloat16 or wider, within the bound.
No kernel may reach another device: no remote copies, remote signals or barrier semaphores. Data moves between devices by JAX's collectives and lax.ppermute only.
A program may use at most 64 MiB of HBM per device.

v0:
```python
import math

import jax
import jax.numpy as jnp
from jax import lax
from jax.sharding import PartitionSpec as P

HIGHEST = lax.Precision.HIGHEST


def shifted(x, axis, by):
    count = lax.axis_size(axis)
    pairs = [(i, i + by) for i in range(count) if 0 <= i + by < count]
    return lax.ppermute(x, axis, pairs)


def dft_tables(radix_rows, span_cols, total_len):
    half_rows = jnp.arange(radix_rows // 2, dtype=jnp.int32)
    freq_rows = jnp.arange(radix_rows, dtype=jnp.int32)
    inner_cols = jnp.arange(span_cols, dtype=jnp.int32)
    first_angle = (freq_rows[:, None] * half_rows[None, :] % radix_rows).astype(jnp.float32) * (
        -2.0 * math.pi / radix_rows
    )
    twist_angle = (freq_rows[:, None] * inner_cols[None, :] % total_len).astype(jnp.float32) * (
        -2.0 * math.pi / total_len
    )
    last_angle = (inner_cols[:, None] * inner_cols[None, :] % span_cols).astype(jnp.float32) * (
        -2.0 * math.pi / span_cols
    )
    return (
        (jnp.cos(first_angle), jnp.sin(first_angle)),
        (jnp.cos(twist_angle), jnp.sin(twist_angle)),
        (jnp.cos(last_angle), jnp.sin(last_angle)),
        total_len,
    )


def forward_transform(signal, tables):
    first, twist, last, total_len = tables
    channels = signal.shape[0]
    half_rows = first[0].shape[1]
    radix_rows = first[0].shape[0]
    span_cols = last[0].shape[0]
    blocks = signal.reshape(channels, half_rows, span_cols)
    part_re = jnp.einsum("ca,kab->kcb", first[0], blocks, precision=HIGHEST)
    part_im = jnp.einsum("ca,kab->kcb", first[1], blocks, precision=HIGHEST)
    turned_re = (part_re * twist[0] - part_im * twist[1]).reshape(-1, span_cols)
    turned_im = (part_re * twist[1] + part_im * twist[0]).reshape(-1, span_cols)
    spec_re = jnp.dot(turned_re, last[0], precision=HIGHEST) - jnp.dot(
        turned_im, last[1], precision=HIGHEST
    )
    spec_im = jnp.dot(turned_re, last[1], precision=HIGHEST) + jnp.dot(
        turned_im, last[0], precision=HIGHEST
    )
    return (
        spec_re.reshape(channels, radix_rows, span_cols),
        spec_im.reshape(channels, radix_rows, span_cols),
    )


def inverse_transform(spec_re, spec_im, tables):
    first, twist, last, total_len = tables
    channels, radix_rows, span_cols = spec_re.shape
    flat_re = spec_re.reshape(-1, span_cols)
    flat_im = spec_im.reshape(-1, span_cols)
    back_re = (
        jnp.dot(flat_re, last[0], precision=HIGHEST) + jnp.dot(flat_im, last[1], precision=HIGHEST)
    ).reshape(channels, radix_rows, span_cols)
    back_im = (
        jnp.dot(flat_im, last[0], precision=HIGHEST) - jnp.dot(flat_re, last[1], precision=HIGHEST)
    ).reshape(channels, radix_rows, span_cols)
    turned_re = back_re * twist[0] + back_im * twist[1]
    turned_im = back_im * twist[0] - back_re * twist[1]
    signal = jnp.einsum("ca,kcb->kab", first[0], turned_re, precision=HIGHEST)
    signal = signal + jnp.einsum("ca,kcb->kab", first[1], turned_im, precision=HIGHEST)
    return signal.reshape(channels, -1) * (1.0 / total_len)


def spectral(gated_in, inner_grad, long_filter, skip_gain, tables, length):
    gated_f = gated_in.astype(jnp.float32)
    d_inner = inner_grad.astype(jnp.float32)
    filter_re, filter_im = forward_transform(long_filter, tables)
    gated_re, gated_im = forward_transform(gated_f, tables)
    long_part = inverse_transform(
        gated_re * filter_re - gated_im * filter_im,
        gated_re * filter_im + gated_im * filter_re,
        tables,
    )
    skip_col = skip_gain[:, None]
    inner_sum = (long_part + skip_col * gated_f).astype(jnp.bfloat16)
    grad_re, grad_im = forward_transform(d_inner, tables)
    corr_filter = inverse_transform(
        filter_re * grad_re + filter_im * grad_im, filter_re * grad_im - filter_im * grad_re, tables
    )
    dgated_c = (corr_filter + skip_col * d_inner).astype(jnp.bfloat16)
    grad_scale = 1.0 / math.sqrt(length)
    d_filter = (
        inverse_transform(
            gated_re * grad_re + gated_im * grad_im, gated_re * grad_im - gated_im * grad_re, tables
        )
        * grad_scale
    )
    d_skip = jnp.sum(d_inner * gated_f, axis=1) * grad_scale
    return (inner_sum, dgated_c, d_filter, d_skip)


def body(query_in, key_in, value_in, short_weights, long_filter, skip_gain, cotangent):
    tok_rows, columns = query_in.shape
    ctx_count = lax.axis_size("ctx")
    length = tok_rows * ctx_count
    tables = dft_tables(2 * ctx_count, tok_rows, 2 * length)
    grad_scale = 1.0 / math.sqrt(length)
    stacked = jnp.stack([query_in, key_in, value_in])
    rim_rows = shifted(stacked[:, tok_rows - 2 :, :], "ctx", 1)
    extended = jnp.concatenate([rim_rows, stacked], axis=1).astype(jnp.float32)
    weights = short_weights[:, :, None, :]
    convolved = (
        weights[:, 0] * extended[:, 2:]
        + weights[:, 1] * extended[:, 1:-1]
        + weights[:, 2] * extended[:, :-2]
    )
    conv_query = lax.optimization_barrier(convolved[0].astype(jnp.bfloat16))
    gated_in = (convolved[1] * convolved[2]).astype(jnp.bfloat16)
    query_f = conv_query.astype(jnp.float32)
    cot_f = cotangent.astype(jnp.float32)
    inner_grad = (cot_f * query_f).astype(jnp.bfloat16)
    gated_c, grad_c = (
        lax.all_to_all(gated_in.T, "ctx", split_axis=0, concat_axis=1, tiled=True),
        lax.all_to_all(inner_grad.T, "ctx", split_axis=0, concat_axis=1, tiled=True),
    )
    inner_c, dgated_c, d_filter, d_skip = spectral(
        gated_c, grad_c, long_filter, skip_gain, tables, length
    )
    inner_t, dgated_t = (
        lax.all_to_all(inner_c, "ctx", split_axis=1, concat_axis=0, tiled=True),
        lax.all_to_all(dgated_c, "ctx", split_axis=1, concat_axis=0, tiled=True),
    )
    inner_f = inner_t.T.astype(jnp.float32)
    mixed_t = (query_f * inner_f).astype(jnp.bfloat16)
    dquery_f = lax.optimization_barrier((cot_f * inner_f).astype(jnp.bfloat16)).astype(jnp.float32)
    dgated_f = dgated_t.T.astype(jnp.float32)
    dstack = jnp.stack([dquery_f, dgated_f * convolved[2], dgated_f * convolved[1]])
    next_rows = shifted(dstack[:, :2, :], "ctx", -1)
    tail_rows = jnp.concatenate([dstack, next_rows], axis=1)
    d_inputs = (
        weights[:, 0] * tail_rows[:, :-2]
        + weights[:, 1] * tail_rows[:, 1:-1]
        + weights[:, 2] * tail_rows[:, 2:]
    ).astype(jnp.bfloat16)
    partial_sums = jnp.stack(
        [
            jnp.sum(dstack * extended[:, 2 - offset : 2 - offset + tok_rows], axis=1)
            for offset in range(3)
        ],
        axis=1,
    )
    d_short = lax.psum(partial_sums, "ctx") * grad_scale
    return (mixed_t, d_inputs[0], d_inputs[1], d_inputs[2], d_filter, d_skip, d_short)


def solution(mesh):
    in_specs = (
        P("ctx", "tp"),
        P("ctx", "tp"),
        P("ctx", "tp"),
        P(None, None, "tp"),
        P(("tp", "ctx"), None),
        P(("tp", "ctx")),
        P("ctx", "tp"),
    )
    out_specs = (
        P("ctx", "tp"),
        P("ctx", "tp"),
        P("ctx", "tp"),
        P("ctx", "tp"),
        P(("tp", "ctx"), None),
        P(("tp", "ctx")),
        P(None, None, "tp"),
    )
    return jax.shard_map(body, mesh=mesh, in_specs=in_specs, out_specs=out_specs, check_vma=False)
```

profile of v0, /device:TPU:24, one launch (start us, length us, event | category | flops | bytes accessed | tf_op | source)
XLA Modules:
  0.0 488.2 jit_solution(10227407453460510825)
XLA Ops:
  4.4 4.6 collective-permute-start
  9.0 2.2 fusion.54
  11.9 4.7 collective-permute-done
  22.6 20.4 %all-to-all-start.2 = ((bf16[64,8,256]{2,1,0:T(8,128)(2,1)}), bf16[64,8,256]{2,1,0:T(8,128)(2,1)S(1)}, u32[]{:S(2)}, u32[]{:S(2)}) async-start(bf16[64,8,256]{2,1,0:T(8,128)(2,1)} %fusion.61), calls=%async_computation.2 | async-start | bytes 524288 | tf_op jit(solution)/shard_map/all_to_all | solution.py:129
  43.1 2.6 multiply_add_fusion.5
  47.7 3.0 convolution_subtract_fusion.4
  51.4 11.8 %all-to-all-done.2 = bf16[64,8,256]{2,1,0:T(8,128)(2,1)S(1)} async-done(((bf16[64,8,256]{2,1,0:T(8,128)(2,1)}), bf16[64,8,256]{2,1,0:T(8,128)(2,1)S(1)}, u32[]{:S(2)}, u32[]{:S(2)}) %all-to-all-start.2) | async-done | bytes 262176 | tf_op jit(solution)/shard_map/all_to_all | solution.py:129
  63.2 6.9 %all-to-all-start = ((bf16[64,8,256]{2,1,0:T(8,128)(2,1)}), bf16[64,8,256]{2,1,0:T(8,128)(2,1)}, u32[]{:S(2)}, u32[]{:S(2)}) async-start(bf16[64,8,256]{2,1,0:T(8,128)(2,1)} %fusion.59), calls=%async_computation | async-start | bytes 524288 | tf_op jit(solution)/shard_map/all_to_all | solution.py:128
  70.1 3.3 fusion.108
  73.4 2.9 convolution_add_fusion.4
  79.8 9.4 %all-to-all-done = bf16[64,8,256]{2,1,0:T(8,128)(2,1)} async-done(((bf16[64,8,256]{2,1,0:T(8,128)(2,1)}), bf16[64,8,256]{2,1,0:T(8,128)(2,1)}, u32[]{:S(2)}, u32[]{:S(2)}) %all-to-all-start) | async-done | bytes 262176 | tf_op jit(solution)/shard_map/all_to_all | solution.py:128
  91.0 2.4 multiply_add_fusion.3
  93.4 2.0 fusion.103
  97.4 2.2 fusion.110
  101.5 2.0 convolution_subtract_fusion.2
  103.5 2.0 convolution_add_fusion.2
  105.5 2.0 convolution_subtract_fusion.5
  107.6 4.8 multiply_add_fusion.1
  123.1 2.2 fusion.89
  127.2 2.0 convolution_subtract_fusion.3
  129.2 2.0 convolution_add_fusion.3
  134.9 7.0 %all-to-all-start.1 = ((bf16[8,64,256]{2,0,1:T(8,128)(2,1)}), bf16[8,64,256]{2,0,1:T(8,128)(2,1)}, u32[]{:S(2)}, u32[]{:S(2)}) async-start(bf16[8,64,256]{2,0,1:T(8,128)(2,1)} %copy.37), calls=%async_computation.1 | async-start | bytes 524288 | tf_op jit(solution)/shard_map/all_to_all | solution.py:135
  142.0 3.3 fusion.80
  147.2 3.0 convolution_add_fusion
  150.2 3.0 convolution_subtract_fusion
  153.2 7.9 %all-to-all-done.1 = bf16[8,64,256]{2,0,1:T(8,128)(2,1)} async-done(((bf16[8,64,256]{2,0,1:T(8,128)(2,1)}), bf16[8,64,256]{2,0,1:T(8,128)(2,1)}, u32[]{:S(2)}, u32[]{:S(2)}) %all-to-all-start.1) | async-done | bytes 262176 | tf_op jit(solution)/shard_map/all_to_all | solution.py:135
  161.1 7.6 %all-to-all-start.3 = ((bf16[8,64,256]{2,0,1:T(8,128)(2,1)}), bf16[8,64,256]{2,0,1:T(8,128)(2,1)}, u32[]{:S(2)}, u32[]{:S(2)}) async-start(bf16[8,64,256]{2,0,1:T(8,128)(2,1)} %copy.40), calls=%async_computation.3 | async-start | bytes 524288 | tf_op jit(solution)/shard_map/all_to_all | solution.py:136
  170.3 3.3 fusion.16
  175.5 11.8 %all-to-all-done.3 = bf16[8,64,256]{2,0,1:T(8,128)(2,1)} async-done(((bf16[8,64,256]{2,0,1:T(8,128)(2,1)}), bf16[8,64,256]{2,0,1:T(8,128)(2,1)}, u32[]{:S(2)}, u32[]{:S(2)}) %all-to-all-start.3) | async-done | bytes 262176 | tf_op jit(solution)/shard_map/all_to_all | solution.py:136
  193.7 2.6 fusion.4
  201.5 3.9 multiply_reduce_fusion.2
  205.4 278.0 %psum.7 = f32[3,3,512]{2,0,1:T(4,128)S(1)} all-reduce(f32[3,3,512]{2,0,1:T(4,128)S(1)} %pad_maximum_fusion.4), channel_id=1, replica_groups=mesh['ctx'=64,'tp'=8] {'ctx'}, use_global_device_ids=true, to_apply=%region_4.5 | all-reduce | flops 4608 | bytes 36864 | tf_op jit(solution)/shard_map/psum | solution.py:157
  (107 shorter events, 60.0 us)
Async XLA Ops:
  0.6 8.4 %copy-start = (f32[8,16384]{1,0:T(8,128)S(1)}, f32[8,16384]{1,0:T(8,128)}, u32[]{:S(2)}) copy-start(f32[8,16384]{1,0:T(8,128)} %param.11) | copy-start | bytes 1572868
  0.6 8.3 %copy-start.25 = (f32[3,3,512]{2,1,0:T(4,128)S(1)}, f32[3,3,512]{2,1,0:T(4,128)}, u32[]{:S(2)}) copy-start(f32[3,3,512]{2,1,0:T(4,128)} %param.10) | copy-start | bytes 55300
  1.8 9.4 %copy-start.21 = (bf16[256,512]{0,1:T(8,128)(2,1)}, bf16[256,512]{0,1:T(8,128)(2,1)S(1)}, u32[]{:S(2)}) copy-start(bf16[256,512]{0,1:T(8,128)(2,1)S(1)} %copy.31) | copy-start | bytes 786436
  3.0 8.2 %copy-start.22 = (bf16[256,512]{0,1:T(8,128)(2,1)}, bf16[256,512]{0,1:T(8,128)(2,1)S(1)}, u32[]{:S(2)}) copy-start(bf16[256,512]{0,1:T(8,128)(2,1)S(1)} %copy.32) | copy-start | bytes 786436
  4.2 7.7 %copy-start.23 = (bf16[256,512]{0,1:T(8,128)(2,1)}, bf16[256,512]{0,1:T(8,128)(2,1)S(1)}, u32[]{:S(2)}) copy-start(bf16[256,512]{0,1:T(8,128)(2,1)S(1)} %copy.33) | copy-start | bytes 786436
  4.2 7.5 %copy-start.24 = (bf16[256,512]{1,0:T(8,128)(2,1)S(1)}, bf16[256,512]{1,0:T(8,128)(2,1)}, u32[]{:S(2)}) copy-start(bf16[256,512]{1,0:T(8,128)(2,1)} %param.13) | copy-start | bytes 786436
  4.4 12.2 %collective-permute-start = (bf16[3,2,512]{1,2,0:T(8,128)(2,1)S(1)}, bf16[3,2,512]{1,2,0:T(8,128)(2,1)}, u32[]{:S(2)}, u32[]{:S(2)}) collective-permute-start(bf16[3,2,512]{1,2,0:T(8,128)(2,1)S(1)} %pad_maximum_fusion.2), channel_id=1, source_target_pairs={{0,8},{8,16},{16,24},{24,32},{32,40},{40,48},{48,56},{56,64},{64,7... | collective-permute-start | bytes 18440 | tf_op jit(solution)/shard_map/ppermute | solution.py:14
  11.9 9.2 %copy-start.17 = (bf16[256,512]{0,1:T(8,128)(2,1)}, bf16[256,512]{0,1:T(8,128)(2,1)S(1)}, u32[]{:S(2)}) copy-start(bf16[256,512]{0,1:T(8,128)(2,1)S(1)} %copy.38) | copy-start | bytes 786436
  19.9 1.2 copy-start.1
  22.6 40.6 %all-to-all-start.2 = ((bf16[64,8,256]{2,1,0:T(8,128)(2,1)}), bf16[64,8,256]{2,1,0:T(8,128)(2,1)S(1)}, u32[]{:S(2)}, u32[]{:S(2)}) async-start(bf16[64,8,256]{2,1,0:T(8,128)(2,1)} %fusion.61), calls=%async_computation.2 | async-start | bytes 524288 | tf_op jit(solution)/shard_map/all_to_all | solution.py:129
  45.7 2.0 copy-start.5
  45.7 5.0 %copy-start.3 = (f32[128,8,256]{2,0,1:T(8,128)}, f32[128,8,256]{2,0,1:T(8,128)S(1)}, u32[]{:S(2)}) copy-start(f32[128,8,256]{2,0,1:T(8,128)S(1)} %get-tuple-element.32) | copy-start | bytes 3145732
  47.7 3.0 copy-start.2
  63.2 26.0 %all-to-all-start = ((bf16[64,8,256]{2,1,0:T(8,128)(2,1)}), bf16[64,8,256]{2,1,0:T(8,128)(2,1)}, u32[]{:S(2)}, u32[]{:S(2)}) async-start(bf16[64,8,256]{2,1,0:T(8,128)(2,1)} %fusion.59), calls=%async_computation | async-start | bytes 524288 | tf_op jit(solution)/shard_map/all_to_all | solution.py:128
  70.1 3.3 copy-start.4
  89.2 1.8 copy-start.14
  105.5 2.0 copy-start.15
  105.5 2.0 copy-start.16
  120.3 1.0 copy-start.26
  134.9 26.2 %all-to-all-start.1 = ((bf16[8,64,256]{2,0,1:T(8,128)(2,1)}), bf16[8,64,256]{2,0,1:T(8,128)(2,1)}, u32[]{:S(2)}, u32[]{:S(2)}) async-start(bf16[8,64,256]{2,0,1:T(8,128)(2,1)} %copy.37), calls=%async_computation.1 | async-start | bytes 524288 | tf_op jit(solution)/shard_map/all_to_all | solution.py:135
  141.9 3.3 copy-start.7
  147.2 3.0 copy-start.6
  161.1 26.2 %all-to-all-start.3 = ((bf16[8,64,256]{2,0,1:T(8,128)(2,1)}), bf16[8,64,256]{2,0,1:T(8,128)(2,1)}, u32[]{:S(2)}, u32[]{:S(2)}) async-start(bf16[8,64,256]{2,0,1:T(8,128)(2,1)} %copy.40), calls=%async_computation.3 | async-start | bytes 524288 | tf_op jit(solution)/shard_map/all_to_all | solution.py:136
  169.8 3.8 copy-start.18
  169.8 3.8 copy-start.20
  187.3 1.4 copy-start.8
  188.7 0.8 copy-start.10
  188.7 1.0 copy-start.12
  192.1 6.1 %collective-permute-start.1 = (f32[3,2,512]{2,1,0:T(2,128)S(1)}, f32[3,2,512]{2,1,0:T(2,128)S(1)}, u32[]{:S(2)}, u32[]{:S(2)}) collective-permute-start(f32[3,2,512]{2,1,0:T(2,128)S(1)} %copy.41), channel_id=1, source_target_pairs={{8,0},{16,8},{24,16},{32,24},{40,32},{48,40},{56,48},{64,56},{72,6... | collective-permute-start | bytes 36872 | tf_op jit(solution)/shard_map/ppermute | solution.py:14
  199.4 1.9 copy-start.9
  199.4 1.9 copy-start.11
  199.4 2.1 copy-start.13
  (1 other events, 0.7 us)
where the time goes:
time: 497 us; the launch traced here: 488 us
  blocking collectives  278 us (56%)
  matrix products  80.2 us (16%)
  starting transfers between devices  48 us (10%)
  waiting for transfers between devices  45.6 us (9%)
  local copies, waits for them, and re-layouts  18.2 us (4%)
  other arithmetic  16.4 us (3%)
    psum x1, blocking collectives, body(): d_short = lax.psum(partial_sums, 'ctx') * grad_scale  278 us
    all_to_all x1, starting transfers between devices, body(): lax.all_to_all(inner_grad.T, 'ctx', split_axis=0, concat_axis=1, tiled=True)  20.4 us
    all_to_all x1, waiting for transfers between devices, body(): lax.all_to_all(dgated_c, 'ctx', split_axis=1, concat_axis=0, tiled=True)  11.8 us
    all_to_all x1, waiting for transfers between devices, body(): lax.all_to_all(inner_grad.T, 'ctx', split_axis=0, concat_axis=1, tiled=True)  11.8 us
    unnamed x66, local copies, waits for them, and re-layouts  11.8 us
  transfers between devices with their start and end apart: 6, of which 5 were waited for; matrix products, arithmetic and copies ran while one was open for 9% of the time, Pallas kernels for 0%

commit v1 on v0

v1 whole, which is shorter than its diff:
```python
import jax
import jax.numpy as jnp
import ml_dtypes
import numpy as np
from jax import lax
from jax.experimental import pallas as pl
from jax.experimental.pallas import tpu as pltpu
from jax.sharding import PartitionSpec as P

ROWS = 128
COLS = 128
LANES = 128
OWN = 8
F32 = jnp.float32
BF16 = jnp.bfloat16
VMEM = pltpu.VMEM


def halves(table):
    high = table.astype(np.float32).astype(ml_dtypes.bfloat16)
    low = (table - high.astype(np.float64)).astype(np.float32).astype(ml_dtypes.bfloat16)
    return high, low


def tables():
    r = np.arange(128, dtype=np.int64)
    full = 4 * ROWS * COLS
    first = 2.0 * np.pi / 512 * ((r[None, :] * (2 * r[:, None] + 1)) % 512)
    turn = -2.0 * np.pi / full * ((r[None, :] * (2 * r[:, None] + 1)) % full)
    last = 2.0 * np.pi / 128 * ((r[:, None] * r[None, :]) % 128)
    w_high, w_low = halves(np.concatenate([np.cos(first), -np.sin(first)], 0))
    t = np.block([[np.cos(last), -np.sin(last)], [np.sin(last), np.cos(last)]])
    t_high, t_low = halves(t)
    i_high, i_low = halves(t.T.copy())
    back = np.concatenate([np.cos(first).T, -np.sin(first).T], 1) * (2.0 / (2 * ROWS * COLS))
    b_high, b_low = halves(back)
    return dict(
        first_pair=np.concatenate([w_high, w_low], 1),
        first_three=np.concatenate([w_high, w_low, w_high], 1),
        turn_re=np.cos(turn).astype(np.float32),
        turn_im=np.sin(turn).astype(np.float32),
        last=np.concatenate([t_high, t_high, t_low], 0),
        last_back=np.concatenate([i_high, i_high, i_low], 0),
        first_back=np.concatenate([b_high, b_low, b_high], 1),
    )


def dot(a, b):
    return jnp.dot(a, b, preferred_element_type=F32)


def split(x):
    high = x.astype(BF16)
    return high, (x - high.astype(F32)).astype(BF16)


def rounded(x):
    return x.astype(BF16).astype(F32)


def wide(x):
    high, low = split(x)
    return jnp.concatenate([high, low, high], axis=1)


def tall(x):
    high, low = split(x)
    return jnp.concatenate([high, high, low], axis=0)


def turned(part, tr, ti):
    re, im = part[:128], part[128:]
    return jnp.concatenate([re * tr - im * ti, re * ti + im * tr], axis=1)


def turned_back(part, tr, ti):
    re, im = part[:, :128], part[:, 128:]
    return jnp.concatenate([re * tr + im * ti, im * tr - re * ti], axis=0)


def pack_kernel(q, k, v, c, out):
    for j in range(4):
        cols = slice(128 * j, 128 * j + 128)
        for top, low, off in ((k, q, 0), (v, c, 256)):
            upper = top[:, cols].astype(F32).T.reshape(16, OWN, 256)
            lower = low[:, cols].astype(F32).T.reshape(16, OWN, 256)
            both = jnp.concatenate([upper, lower], axis=1)
            out[16 * j : 16 * j + 16, :, off : off + 256] = both.astype(BF16)


def filter_kernel(f, first, tr, ti, last, out, rows):
    for a in range(ROWS):
        rows[8 * a : 8 * a + 8, :] = f[:, 128 * a : 128 * a + 128]
    for p in range(OWN // 2):
        x = jnp.concatenate(
            [rows[pl.ds(2 * p + i, ROWS, stride=OWN), :] for i in range(2)], axis=1
        )
        part = dot(first[...], tall(x))
        lhs = jnp.concatenate(
            [turned(part[:, 128 * i : 128 * i + 128], tr[...], ti[...]) for i in range(2)], axis=0
        )
        spec = dot(wide(lhs), last[...])
        out[2 * p] = spec[:128]
        out[2 * p + 1] = spec[128:]


def lagged(x, lane, by):
    r = pltpu.roll(x, by, axis=2)
    return jnp.where(lane < by, r[1:9], r[2:10])


def channel_kernel(
    x, w, skip, filt, first, tr, ti, last, last_back, first_back,
    out, cross, dskip,
    gated_s, grad_s, inner_s, corr_s, cot_s, conv_s, raw_s,
):
    lane = lax.broadcasted_iota(jnp.int32, (8, OWN, LANES), 2)
    scale = 1.0 / 128.0

    def blocks(value, upper, off):
        rows = slice(0, 8) if upper else slice(8, 16)
        lo = value[:, rows, off : off + 128]
        hi = value[:, rows, off + 128 : off + 256]
        return jnp.stack([lo, hi], axis=1).reshape(-1, OWN, LANES)

    def convolve(i, carry):
        s0 = 4 * i
        keep = jnp.where(i > 0, 1.0, 0.0).astype(F32)
        before = x[pl.ds(jnp.maximum(s0 - 1, 0), 1)].astype(F32) * keep
        here = x[pl.ds(s0, 4)].astype(F32)
        value = jnp.concatenate([before, here], axis=0)
        at = pl.ds(8 * i, 8)
        convs = []
        for s, (upper, off) in enumerate(((False, 0), (True, 0), (True, 256))):
            seq = blocks(value, upper, off)
            lags = [seq[2:], lagged(seq, lane, 1), lagged(seq, lane, 2)]
            for j in range(3):
                raw_s[3 * s + j, at] = lags[j]
            convs.append(
                w[3 * s] * lags[0] + w[3 * s + 1] * lags[1] + w[3 * s + 2] * lags[2]
            )
        cot = blocks(here, False, 256)
        cot_s[at] = cot
        conv_s[0, at] = convs[1]
        conv_s[1, at] = convs[2]
        flat = pl.ds(64 * i, 64)
        gated_s[flat, :] = rounded(convs[1] * convs[2]).reshape(64, LANES)
        grad_s[flat, :] = rounded(cot * rounded(convs[0])).reshape(64, LANES)
        return carry

    lax.fori_loop(0, 16, convolve, 0)

    for ch in range(OWN):
        own = pl.ds(ch, ROWS, stride=OWN)
        pair = jnp.concatenate([gated_s[own, :], grad_s[own, :]], axis=1).astype(BF16)
        part = dot(first[...], jnp.concatenate([pair, pair], axis=0))
        lhs = jnp.concatenate(
            [turned(part[:, 128 * i : 128 * i + 128], tr[...], ti[...]) for i in range(2)], axis=0
        )
        spec = dot(wide(lhs), last[...])
        gr, gi = spec[:128, :128], spec[:128, 128:]
        dr, di = spec[128:, :128], spec[128:, 128:]
        fr, fi = filt[ch][:, :128], filt[ch][:, 128:]
        cross[ch] = jnp.concatenate([gr * dr + gi * di, gr * di - gi * dr], axis=1)
        inner = jnp.concatenate([gr * fr - gi * fi, gr * fi + gi * fr], axis=1)
        corr = jnp.concatenate([fr * dr + fi * di, fr * di - fi * dr], axis=1)
        back = dot(wide(jnp.concatenate([inner, corr], axis=0)), last_back[...])
        turn = jnp.concatenate(
            [turned_back(back[128 * i : 128 * i + 128], tr[...], ti[...]) for i in range(2)], axis=1
        )
        y = dot(first_back[...], tall(turn))
        inner_s[own, :] = y[:, :128]
        corr_s[own, :] = y[:, 128:]

    def finish(i, sums):
        at = pl.ds(8 * i, 8)
        flat = pl.ds(64 * i, 64)
        gated = gated_s[flat, :].reshape(8, OWN, LANES)
        grad = grad_s[flat, :].reshape(8, OWN, LANES)
        inner = rounded(inner_s[flat, :].reshape(8, OWN, LANES) + skip[...] * gated)
        dgated = rounded(corr_s[flat, :].reshape(8, OWN, LANES) + skip[...] * grad)
        dconv = (rounded(cot_s[at] * inner), dgated * conv_s[1, at], dgated * conv_s[0, at])
        terms = [dconv[s] * raw_s[3 * s + j, at] for s in range(3) for j in range(3)]
        terms.append(grad * gated)
        sums = tuple(total + jnp.sum(term, axis=0) for total, term in zip(sums, terms))
        for value, off in ((dgated, 0), (inner, 256)):
            value = value.reshape(4, 2, OWN, LANES)
            both = jnp.concatenate([value[:, 0], value[:, 1]], axis=2)
            out[pl.ds(4 * i, 4), :, off : off + 256] = both.astype(BF16)
        return sums

    zero = jnp.zeros((OWN, LANES), F32)
    sums = lax.fori_loop(0, 16, finish, (zero,) * 10)
    totals = [jnp.sum(total, axis=1, keepdims=True) * scale for total in sums]
    dskip[...] = jnp.broadcast_to(totals[9], (OWN, LANES))

    spot = lax.broadcasted_iota(jnp.int32, (OWN, LANES), 1)
    shared = zero
    for n in range(9):
        value = jnp.broadcast_to(totals[n], (OWN, LANES))
        high = rounded(value)
        mid = rounded(value - high)
        for base, piece in ((0, high), (16, mid), (32, value - high - mid)):
            shared = jnp.where(spot == base + n, piece, shared)
    for g in range(4):
        s0 = 16 * g
        edge = []
        for off, by in ((0, 48), (256, 50)):
            if g < 3:
                after = out[s0 : s0 + 32, :, off : off + 128].astype(F32)[1:17]
            else:
                after = out[s0 : s0 + 16, :, off : off + 128].astype(F32)
                after = jnp.concatenate([after[1:], jnp.zeros((1, OWN, LANES), F32)], axis=0)
            edge.append(pltpu.roll(after, by, axis=2))
        rest = jnp.where(spot < 50, edge[0], edge[1])
        extra = jnp.where(spot < 48, shared, jnp.where(spot < 52, rest, 0.0))
        out[s0 : s0 + 16, :, 512:640] = extra.astype(BF16)


def cross_kernel(cross, tr, ti, last_back, first_back, out, rows):
    for p in range(OWN // 2):
        both = jnp.concatenate([cross[2 * p], cross[2 * p + 1]], axis=0)
        back = dot(wide(both), last_back[...])
        turn = jnp.concatenate(
            [turned_back(back[128 * i : 128 * i + 128], tr[...], ti[...]) for i in range(2)], axis=1
        )
        y = dot(first_back[...], tall(turn)) * (1.0 / 128.0)
        for i in range(2):
            rows[pl.ds(2 * p + i, ROWS, stride=OWN), :] = y[:, 128 * i : 128 * i + 128]
    for a in range(ROWS):
        out[:, 128 * a : 128 * a + 128] = rows[8 * a : 8 * a + 8, :]


def token_kernel(got, q, k, v, c, prev, nxt, w, mixed, dq, dk, dv, dshort):
    for j in range(4):
        cols = slice(128 * j, 128 * j + 128)
        own = slice(16 * j, 16 * j + 16)

        def columns(off, width):
            return got[own, :, off : off + width].astype(F32).reshape(128, width).T

        dgated = columns(0, 256)
        inner = columns(256, 256)
        extra = columns(512, 128)
        for s in range(3):
            for n in range(3):
                at = 3 * s + n
                total = extra[at : at + 1] + extra[16 + at : 17 + at] + extra[32 + at : 33 + at]
                dshort[s, n : n + 1, cols] = total
        weight = [[w[s, n : n + 1, cols] for n in range(3)] for s in range(3)]
        cot = c[:, cols].astype(F32)
        cot_n = nxt[4:6, cols]

        def conv(seq, s):
            rows = seq.shape[0] - 2
            return (
                weight[s][0] * seq[2:] + weight[s][1] * seq[1 : 1 + rows] + weight[s][2] * seq[:rows]
            )

        def back(seq, s):
            total = (
                weight[s][0] * seq[:256] + weight[s][1] * seq[1:257] + weight[s][2] * seq[2:258]
            )
            return total.astype(BF16)

        q_ext = jnp.concatenate([prev[0:2, cols], q[:, cols].astype(F32)], axis=0)
        query = rounded(conv(q_ext, 0))
        mixed[:, cols] = (query * inner).astype(BF16)
        dconv = jnp.concatenate([rounded(cot * inner), rounded(cot_n * extra[50:52])], axis=0)
        dq[:, cols] = back(dconv, 0)
        dgated_ext = jnp.concatenate([dgated, extra[48:50]], axis=0)
        k_ext = jnp.concatenate([prev[2:4, cols], k[:, cols].astype(F32), nxt[0:2, cols]], axis=0)
        v_ext = jnp.concatenate([prev[4:6, cols], v[:, cols].astype(F32), nxt[2:4, cols]], axis=0)
        dk[:, cols] = back(dgated_ext * conv(v_ext, 2), 1)
        dv[:, cols] = back(dgated_ext * conv(k_ext, 1), 2)


def call(kernel, outs, scratch=(), flops=0, moved=0, limit=24):
    one = not isinstance(outs, list)
    shapes = [outs] if one else outs
    return pl.pallas_call(
        kernel,
        out_shape=shapes[0] if one else shapes,
        scratch_shapes=list(scratch),
        compiler_params=pltpu.CompilerParams(vmem_limit_bytes=limit << 20),
        cost_estimate=pl.CostEstimate(flops=flops, bytes_accessed=moved, transcendentals=0),
    )


def shape(*dims, kind=F32):
    return jax.ShapeDtypeStruct(dims, kind)


def body(query_in, key_in, value_in, short_weights, long_filter, skip_gain, cotangent):
    t = tables()
    turns = (t["turn_re"], t["turn_im"])
    count = lax.axis_size("ctx")
    here = lax.axis_index("ctx")

    packed = call(pack_kernel, shape(64, 16, 512, kind=BF16), moved=2 << 20)(
        query_in, key_in, value_in, cotangent
    )
    seqs = lax.all_to_all(packed, "ctx", split_axis=0, concat_axis=0, tiled=True)

    spectrum = call(
        filter_kernel, shape(OWN, 128, 256), [VMEM((1024, LANES), F32)],
        flops=10**9, moved=2 << 20,
    )(long_filter, t["first_three"], *turns, t["last"])

    ends = jnp.concatenate([query_in[254:], key_in[254:], value_in[254:]], axis=0)
    starts = jnp.concatenate([key_in[:2], value_in[:2], cotangent[:2]], axis=0)
    prev = lax.ppermute(ends, "ctx", [(i, i + 1) for i in range(count - 1)]).astype(F32)
    nxt = lax.ppermute(starts, "ctx", [(i + 1, i) for i in range(count - 1)]).astype(F32)

    own_w = lax.dynamic_slice_in_dim(short_weights, OWN * here, OWN, axis=2).reshape(9, OWN, 1)
    own_w = jnp.broadcast_to(own_w, (9, OWN, LANES))
    own_skip = jnp.broadcast_to(skip_gain[:, None], (OWN, LANES))

    big = VMEM((128, OWN, LANES), F32)
    flat = VMEM((1024, LANES), F32)
    answer, cross, dskip = call(
        channel_kernel,
        [shape(64, OWN, 640, kind=BF16), shape(OWN, 128, 256), shape(OWN, LANES)],
        [flat, flat, flat, flat, big, VMEM((2, 128, OWN, LANES), F32), VMEM((9, 128, OWN, LANES), F32)],
        flops=4 * 10**9, moved=4 << 20,
    )(seqs, own_w, own_skip, spectrum, t["first_pair"], *turns, t["last"], t["last_back"], t["first_back"])

    got = lax.all_to_all(answer, "ctx", split_axis=0, concat_axis=0, tiled=True)

    d_filter = call(
        cross_kernel, shape(OWN, 16384), [flat], flops=10**9, moved=2 << 20
    )(cross, *turns, t["last_back"], t["first_back"])

    tokens = shape(256, 512, kind=BF16)
    mixed, d_query, d_key, d_value, d_short = call(
        token_kernel, [tokens, tokens, tokens, tokens, shape(3, 3, 512)], moved=3 << 20
    )(got, query_in, key_in, value_in, cotangent, prev, nxt, short_weights)
    return (mixed, d_query, d_key, d_value, d_filter, dskip[:, 0], d_short)


def solution(mesh):
    tokens = P("ctx", "tp")
    rows = P(("tp", "ctx"), None)
    taps = P(None, None, "tp")
    flat = P(("tp", "ctx"))
    in_specs = (tokens, tokens, tokens, taps, rows, flat, tokens)
    out_specs = (tokens, tokens, tokens, tokens, rows, flat, taps)
    return jax.shard_map(body, mesh=mesh, in_specs=in_specs, out_specs=out_specs, check_vma=False)
```

time: 497 us -> 137 us (0.28); the launches traced: 488 us -> 137 us
  blocking collectives: 278 us -> 0 us
  matrix products: 80.2 us -> 0 us
  waiting for transfers between devices: 45.6 us -> 78.3 us
  starting transfers between devices: 48 us -> 30.4 us
  Pallas kernels: 0 us -> 17.3 us
  other arithmetic: 16.4 us -> 0.03 us
  local copies, waits for them, and re-layouts: 18.2 us -> 9.81 us
    psum x1 -> x0, blocking collectives: 278 us -> none  [body(): d_short = lax.psum(partial_sums, 'ctx') * grad_scale]
    dot_general x36 -> x0, matrix products: 80.2 us -> none  [the longest x3 9.69 us: forward_transform(): jnp.dot(turned_im, last[0], precision=HIGHEST)]
    ppermute x2, waiting for transfers between devices: 4.66 us -> 22.5 us  [the longest x1 17.2 us: body(): lax.ppermute(ends, 'ctx', [(i, i + 1) for i in range(count - 1)])]
    pallas_call x0 -> x5, Pallas kernels: none -> 17.3 us  [the longest x1 9.13 us: body(): call(channel_kernel, [shape(64, OWN, 640, kind=BF16), shape(OWN, 128, 256...]
    all_to_all x4 -> x2, starting transfers between devices: 41.9 us -> 25.6 us  [the longest x1 18.7 us: body(): lax.all_to_all(packed, 'ctx', split_axis=0, concat_axis=0, tiled=True)]
    all_to_all x4 -> x2, waiting for transfers between devices: 40.9 us -> 55.8 us  [the longest x1 51.3 us: body(): lax.all_to_all(packed, 'ctx', split_axis=0, concat_axis=0, tiled=True)]
    reduce_sum x2 -> x0, other arithmetic: 5.04 us -> none  [the longest x1 3.9 us: body(): jnp.sum(dstack * extended[:, 2 - offset:2 - offset + tok_rows], axis=1)]
    unnamed x66 -> x44, local copies, waits for them, and re-layouts: 11.8 us -> 8.26 us
  transfers between devices with their start and end apart: 6 -> 4, of which waited for: 5 -> 4; matrix products, arithmetic and copies ran while one was open for 9% -> 1% of each run, Pallas kernels for 0% -> 3%
where the time goes in v1:
time: 137 us
  waiting for transfers between devices  78.3 us (57%)
  starting transfers between devices  30.4 us (22%)
  Pallas kernels  17.3 us (13%)
  local copies, waits for them, and re-layouts  9.81 us (7%)
    all_to_all x1, waiting for transfers between devices, body(): lax.all_to_all(packed, 'ctx', split_axis=0, concat_axis=0, tiled=True)  51.3 us
    all_to_all x1, starting transfers between devices, body(): lax.all_to_all(packed, 'ctx', split_axis=0, concat_axis=0, tiled=True)  18.7 us
    ppermute x1, waiting for transfers between devices, body(): lax.ppermute(ends, 'ctx', [(i, i + 1) for i in range(count - 1)])  17.2 us
    pallas_call x1, Pallas kernels, body(): call(channel_kernel, [shape(64, OWN, 640, kind=BF16), shape(OWN, 128, 256...  9.13 us
    unnamed x44, local copies, waits for them, and re-layouts  8.26 us
    all_to_all x1, starting transfers between devices, body(): got = lax.all_to_all(answer, 'ctx', split_axis=0, concat_axis=0, tiled=True)  6.91 us
    ppermute x1, waiting for transfers between devices, body(): lax.ppermute(starts, 'ctx', [(i + 1, i) for i in range(count - 1)])  5.31 us
    all_to_all x1, waiting for transfers between devices, body(): got = lax.all_to_all(answer, 'ctx', split_axis=0, concat_axis=0, tiled=True)  4.5 us
  transfers between devices with their start and end apart: 4, of which 4 were waited for; matrix products, arithmetic and copies ran while one was open for 1% of the time, Pallas kernels for 3%

profile of v1, /device:TPU:24, one launch (start us, length us, event | category | flops | bytes accessed | tf_op | source)
XLA Modules:
  0.0 136.7 jit_solution(17333528591834293568)
XLA Ops:
  0.6 0.9 copy-done
  1.6 0.9 copy-done.2
  2.5 0.9 copy-done.4
  3.5 0.9 copy-done.6
  4.4 1.3 shard_map.189
  5.8 0.0 copy-start.15
  5.8 0.0 copy-start.16
  5.8 18.7 %all-to-all-start = ((bf16[64,16,512]{2,1,0:T(8,128)(2,1)}), bf16[64,16,512]{2,1,0:T(8,128)(2,1)S(1)}, u32[]{:S(2)}, u32[]{:S(2)}) async-start(bf16[64,16,512]{2,1,0:T(8,128)(2,1)} %shard_map.189), calls=%async_computation | async-start | bytes 2097152 | tf_op jit(solution)/shard_map/all_to_all | solution.py:303
  24.5 0.1 constant_dynamic-slice_fusion
  24.7 0.0 copy-start.10
  24.7 0.0 copy-start.12
  24.7 0.0 copy-start.14
  24.7 1.4 %shard_map.190.filt = f32[8,128,256]{2,1,0:T(8,128)S(1)} custom-call(f32[8,16384]{1,0:T(8,128)S(1)} %copy-done.9, bf16[256,384]{1,0:T(8,128)(2,1)S(1)} %copy-done.13, f32[128,128]{1,0:T(8,128)S(1)} %copy-done.15, f32[128,128]{1,0:T(8,128)S(1)} %copy-done.16, bf16[768,256]{1,0:T(8,128)(2,1)S(1)} %copy-done.11), custom_call_target="tpu_custom_call" | custom-call | flops 1000000000 | bytes 2097152 | tf_op jit(solution)/shard_map/pallas_call | solution.py:305
  26.1 1.0 copy-done.19
  27.1 51.3 %all-to-all-done.x = bf16[64,16,512]{2,1,0:T(8,128)(2,1)S(1)} async-done(((bf16[64,16,512]{2,1,0:T(8,128)(2,1)}), bf16[64,16,512]{2,1,0:T(8,128)(2,1)S(1)}, u32[]{:S(2)}, u32[]{:S(2)}) %all-to-all-start) | async-done | bytes 1048608 | tf_op jit(solution)/shard_map/all_to_all | solution.py:303
  78.4 0.1 broadcast_in_dim.14.w
  78.4 0.1 broadcast_in_dim.15.skip
  78.5 1.2 copy-done.20
  79.8 9.1 %shard_map.191 = (bf16[64,8,640]{2,1,0:T(8,128)(2,1)}, f32[8,128,256]{2,1,0:T(8,128)S(1)}, f32[8,128]{1,0:T(8,128)S(1)}) custom-call(bf16[64,16,512]{2,1,0:T(8,128)(2,1)S(1)} %all-to-all-done.x, f32[9,8,128]{2,1,0:T(8,128)S(1)} %broadcast_in_dim.14.w, f32[8,128]{1,0:T(8,128)S(1)} %broadcast_in_dim.15.skip, f32[8,128,256]{2,1,0:T(8,128)S(1)} %copy-done.20, ...), custom_call_target="tpu_custom_call" | custom-call | flops 4000000000 | bytes 4194304 | tf_op jit(solution)/shard_map/pallas_call | solution.py:321
  88.9 1.0 copy-done.17
  89.9 6.9 %all-to-all-start.1 = ((bf16[64,8,640]{2,1,0:T(8,128)(2,1)}), bf16[64,8,640]{2,1,0:T(8,128)(2,1)S(1)}, u32[]{:S(2)}, u32[]{:S(2)}) async-start(bf16[64,8,640]{2,1,0:T(8,128)(2,1)} %get-tuple-element.15), calls=%async_computation.1 | async-start | bytes 1310720 | tf_op jit(solution)/shard_map/all_to_all | solution.py:328
  96.9 3.5 %collective-permute-start = (bf16[6,512]{1,0:T(8,128)(2,1)S(1)}, bf16[6,512]{1,0:T(8,128)(2,1)S(1)}, u32[]{:S(2)}, u32[]{:S(2)}) collective-permute-start(bf16[6,512]{1,0:T(8,128)(2,1)S(1)} %pad_maximum_fusion), channel_id=1, source_target_pairs={{0,8},{8,16},{16,24},{24,32},{32,40},{40,48},{48,56},{56,64},{64,7... | collective-permute-start | bytes 18440 | tf_op jit(solution)/shard_map/ppermute | solution.py:312
  100.4 0.0 slice-start
  100.4 0.7 slice-done
  101.1 1.3 collective-permute-start.1
  102.4 17.2 %collective-permute-done = bf16[6,512]{1,0:T(8,128)(2,1)S(1)} collective-permute-done((bf16[6,512]{1,0:T(8,128)(2,1)S(1)}, bf16[6,512]{1,0:T(8,128)(2,1)S(1)}, u32[]{:S(2)}, u32[]{:S(2)}) %collective-permute-start) | collective-permute-done | bytes 6176 | tf_op jit(solution)/shard_map/ppermute | solution.py:312
  119.5 5.3 %collective-permute-done.1 = bf16[6,512]{1,0:T(8,128)(2,1)S(1)} collective-permute-done((bf16[6,512]{1,0:T(8,128)(2,1)S(1)}, bf16[6,512]{1,0:T(8,128)(2,1)S(1)}, u32[]{:S(2)}, u32[]{:S(2)}) %collective-permute-start.1) | collective-permute-done | bytes 6176 | tf_op jit(solution)/shard_map/ppermute | solution.py:313
  124.8 1.2 copy-done.18
  126.1 2.7 %shard_map.193 = f32[8,16384]{1,0:T(8,128)} custom-call(f32[8,128,256]{2,1,0:T(8,128)S(1)} %copy-done.18, f32[128,128]{1,0:T(8,128)S(1)} %copy-done.15, f32[128,128]{1,0:T(8,128)S(1)} %copy-done.16, bf16[768,256]{1,0:T(8,128)(2,1)S(1)} %copy-done.10, bf16[128,768]{1,0:T(8,128)(2,1)S(1)} %copy-done.12), custom_call_target="tpu_custom_call" | custom-call | flops 1000000000 | bytes 2097152 | tf_op jit(solution)/shard_map/pallas_call | solution.py:330
  128.8 0.6 slice_reduce_fusion
  129.4 4.5 %all-to-all-done.1.got = bf16[64,8,640]{2,1,0:T(8,128)(2,1)S(1)} async-done(((bf16[64,8,640]{2,1,0:T(8,128)(2,1)}), bf16[64,8,640]{2,1,0:T(8,128)(2,1)S(1)}, u32[]{:S(2)}, u32[]{:S(2)}) %all-to-all-start.1) | async-done | bytes 655392 | tf_op jit(solution)/shard_map/all_to_all | solution.py:328
  133.9 2.7 %shard_map.192 = (bf16[256,512]{1,0:T(8,128)(2,1)}, bf16[256,512]{1,0:T(8,128)(2,1)}, bf16[256,512]{1,0:T(8,128)(2,1)}, bf16[256,512]{1,0:T(8,128)(2,1)}, f32[3,3,512]{2,1,0:T(4,128)}) custom-call(bf16[64,8,640]{2,1,0:T(8,128)(2,1)S(1)} %all-to-all-done.1.got, bf16[256,512]{1,0:T(8,128)(2,1)S(1)} %copy-done.5, bf16[256,512]{1,0:T(8,128)(2,1)S(1)} %copy-done.1, ...), custom_call_target="tpu_custom_call" | custom-call | bytes 3145728 | tf_op jit(solution)/shard_map/pallas_call | solution.py:335
  (38 shorter events, 0.1 us)
Async XLA Ops:
  0.6 1.0 copy-start
  1.6 0.9 copy-start.2
  2.5 0.9 copy-start.4
  3.5 0.9 copy-start.6
  5.8 18.8 %copy-start.8 = (f32[3,3,512]{2,1,0:T(4,128)S(1)}, f32[3,3,512]{2,1,0:T(4,128)}, u32[]{:S(2)}) copy-start(f32[3,3,512]{2,1,0:T(4,128)} %w.1) | copy-start | bytes 55300
  5.8 18.9 %copy-start.9 = (f32[8,16384]{1,0:T(8,128)S(1)}, f32[8,16384]{1,0:T(8,128)}, u32[]{:S(2)}) copy-start(f32[8,16384]{1,0:T(8,128)} %f.1) | copy-start | bytes 1572868
  5.8 18.9 %copy-start.11 = (bf16[768,256]{1,0:T(8,128)(2,1)S(1)}, bf16[768,256]{1,0:T(8,128)(2,1)}, u32[]{:S(2)}) copy-start(bf16[768,256]{1,0:T(8,128)(2,1)} %constant.29.clone.last) | copy-start | bytes 1179652
  5.8 18.9 %copy-start.13 = (bf16[256,384]{1,0:T(8,128)(2,1)S(1)}, bf16[256,384]{1,0:T(8,128)(2,1)}, u32[]{:S(2)}) copy-start(bf16[256,384]{1,0:T(8,128)(2,1)} %constant.26.clone.first) | copy-start | bytes 589828
  5.8 18.9 %copy-start.15 = (f32[128,128]{1,0:T(8,128)S(1)}, f32[128,128]{1,0:T(8,128)}, u32[]{:S(2)}) copy-start(f32[128,128]{1,0:T(8,128)} %constant.27.clone.tr) | copy-start | bytes 196612
  5.8 18.9 %copy-start.16 = (f32[128,128]{1,0:T(8,128)S(1)}, f32[128,128]{1,0:T(8,128)}, u32[]{:S(2)}) copy-start(f32[128,128]{1,0:T(8,128)} %constant.28.clone.ti) | copy-start | bytes 196612
  5.8 72.6 %all-to-all-start = ((bf16[64,16,512]{2,1,0:T(8,128)(2,1)}), bf16[64,16,512]{2,1,0:T(8,128)(2,1)S(1)}, u32[]{:S(2)}, u32[]{:S(2)}) async-start(bf16[64,16,512]{2,1,0:T(8,128)(2,1)} %shard_map.189), calls=%async_computation | async-start | bytes 2097152 | tf_op jit(solution)/shard_map/all_to_all | solution.py:303
  24.7 53.9 %copy-start.10 = (bf16[768,256]{1,0:T(8,128)(2,1)S(1)}, bf16[768,256]{1,0:T(8,128)(2,1)}, u32[]{:S(2)}) copy-start(bf16[768,256]{1,0:T(8,128)(2,1)} %constant.31.clone.last_back) | copy-start | bytes 1179652
  24.7 53.8 %copy-start.12 = (bf16[128,768]{1,0:T(8,128)(2,1)S(1)}, bf16[128,768]{1,0:T(8,128)(2,1)}, u32[]{:S(2)}) copy-start(bf16[128,768]{1,0:T(8,128)(2,1)} %constant.32.clone.first_back) | copy-start | bytes 589828
  24.7 53.8 %copy-start.14 = (bf16[256,256]{1,0:T(8,128)(2,1)S(1)}, bf16[256,256]{1,0:T(8,128)(2,1)}, u32[]{:S(2)}) copy-start(bf16[256,256]{1,0:T(8,128)(2,1)} %constant.30.clone.first) | copy-start | bytes 393220
  26.1 1.0 copy-start.19
  27.1 51.4 %copy-start.21 = (f32[8]{0:T(128)S(1)}, f32[8]{0:T(128)}, u32[]{:S(2)}) copy-start(f32[8]{0:T(128)} %param.19) | copy-start | bytes 100
  78.5 1.2 copy-start.20
  88.9 1.0 copy-start.17
  89.9 6.9 %copy-start.5 = (bf16[256,512]{1,0:T(8,128)(2,1)S(1)}, bf16[256,512]{1,0:T(8,128)(2,1)}, u32[]{:S(2)}) copy-start(bf16[256,512]{1,0:T(8,128)(2,1)} %q.3) | copy-start | bytes 786436
  89.9 6.9 %copy-start.1 = (bf16[256,512]{1,0:T(8,128)(2,1)S(1)}, bf16[256,512]{1,0:T(8,128)(2,1)}, u32[]{:S(2)}) copy-start(bf16[256,512]{1,0:T(8,128)(2,1)} %k.3) | copy-start | bytes 786436
  89.9 7.0 %copy-start.3 = (bf16[256,512]{1,0:T(8,128)(2,1)S(1)}, bf16[256,512]{1,0:T(8,128)(2,1)}, u32[]{:S(2)}) copy-start(bf16[256,512]{1,0:T(8,128)(2,1)} %v.3) | copy-start | bytes 786436
  89.9 44.1 %all-to-all-start.1 = ((bf16[64,8,640]{2,1,0:T(8,128)(2,1)}), bf16[64,8,640]{2,1,0:T(8,128)(2,1)S(1)}, u32[]{:S(2)}, u32[]{:S(2)}) async-start(bf16[64,8,640]{2,1,0:T(8,128)(2,1)} %get-tuple-element.15), calls=%async_computation.1 | async-start | bytes 1310720 | tf_op jit(solution)/shard_map/all_to_all | solution.py:328
  96.9 22.6 %collective-permute-start = (bf16[6,512]{1,0:T(8,128)(2,1)S(1)}, bf16[6,512]{1,0:T(8,128)(2,1)S(1)}, u32[]{:S(2)}, u32[]{:S(2)}) collective-permute-start(bf16[6,512]{1,0:T(8,128)(2,1)S(1)} %pad_maximum_fusion), channel_id=1, source_target_pairs={{0,8},{8,16},{16,24},{24,32},{32,40},{40,48},{48,56},{56,64},{64,7... | collective-permute-start | bytes 18440 | tf_op jit(solution)/shard_map/ppermute | solution.py:312
  100.4 0.7 slice-start
  101.1 23.8 %collective-permute-start.1 = (bf16[6,512]{1,0:T(8,128)(2,1)S(1)}, bf16[6,512]{1,0:T(8,128)(2,1)S(1)}, u32[]{:S(2)}, u32[]{:S(2)}) collective-permute-start(bf16[6,512]{1,0:T(8,128)(2,1)S(1)} %pad_maximum_fusion.1), channel_id=1, source_target_pairs={{8,0},{16,8},{24,16},{32,24},{40,32},{48,40},{56,48},{64,56},{72,6... | collective-permute-start | bytes 18440 | tf_op jit(solution)/shard_map/ppermute | solution.py:313
  124.8 1.2 copy-start.18
  126.1 7.9 %copy-start.7 = (bf16[256,512]{1,0:T(8,128)(2,1)S(1)}, bf16[256,512]{1,0:T(8,128)(2,1)}, u32[]{:S(2)}) copy-start(bf16[256,512]{1,0:T(8,128)(2,1)} %c.3) | copy-start | bytes 786436

commit v2 on v1

--- a/solution.py
+++ b/solution.py
@@ -14,6 +14,11 @@
 F32 = jnp.float32
 BF16 = jnp.bfloat16
 VMEM = pltpu.VMEM
+HBM = pl.BlockSpec(memory_space=pltpu.HBM)
+WHOLE = pl.BlockSpec(memory_space=pltpu.VMEM)
+GROUP = 4
+SPARE = 24
+TAIL = 2048
 
 
 def halves(table):
@@ -78,17 +83,39 @@
     return jnp.concatenate([re * tr + im * ti, im * tr - re * ti], axis=0)
 
 
-def pack_kernel(q, k, v, c, out):
+def copy(source, target, sem):
+    return pltpu.make_async_copy(source, target, sem)
+
+
+def pack_kernel(q, k, v, c, out, q_v, k_v, v_v, c_v, out_v, sems):
+    loads = [copy(a, b, sems.at[i]) for i, (a, b) in enumerate(((k, k_v), (q, q_v), (v, v_v), (c, c_v)))]
+    for load in loads:
+        load.start()
+    stores = []
+    for load in loads:
+        load.wait()
     for j in range(4):
         cols = slice(128 * j, 128 * j + 128)
-        for top, low, off in ((k, q, 0), (v, c, 256)):
+        for top, low, off in ((k_v, q_v, 0), (v_v, c_v, 256)):
             upper = top[:, cols].astype(F32).T.reshape(16, OWN, 256)
             lower = low[:, cols].astype(F32).T.reshape(16, OWN, 256)
             both = jnp.concatenate([upper, lower], axis=1)
-            out[16 * j : 16 * j + 16, :, off : off + 256] = both.astype(BF16)
-
-
-def filter_kernel(f, first, tr, ti, last, out, rows):
+            out_v[16 * j : 16 * j + 16, :, off : off + 256] = both.astype(BF16)
+        part = pl.ds(16 * j, 16)
+        stores.append(copy(out_v.at[part], out.at[part], sems.at[4 + j]))
+        stores[j].start()
+    for store in stores:
+        store.wait()
+
+
+def filter_kernel(here, f, w, skip, first, tr, ti, last, out, own_w, rows):
+    wanted = OWN * here[0] + lax.broadcasted_iota(jnp.int32, (OWN, 512), 0)
+    mine = lax.broadcasted_iota(jnp.int32, (OWN, 512), 1) == wanted
+    for s in range(3):
+        for n in range(3):
+            value = jnp.sum(jnp.where(mine, w[s, n : n + 1, :], 0.0), axis=1, keepdims=True)
+            own_w[3 * s + n] = jnp.broadcast_to(value, (OWN, LANES))
+    own_w[9] = jnp.broadcast_to(skip[...], (OWN, LANES))
     for a in range(ROWS):
         rows[8 * a : 8 * a + 8, :] = f[:, 128 * a : 128 * a + 128]
     for p in range(OWN // 2):
@@ -110,10 +137,12 @@
 
 
 def channel_kernel(
-    x, w, skip, filt, first, tr, ti, last, last_back, first_back,
+    x, w, filt, first, tr, ti, last, last_back, first_back,
     out, cross, dskip,
-    gated_s, grad_s, inner_s, corr_s, cot_s, conv_s, raw_s,
+    gated_s, grad_s, inner_s, corr_s, cot_s, conv_s, raw_s, edge_s, filt_v, cross_v, out_v, sems,
 ):
+    load = copy(filt.at[pl.ds(0, OWN)], filt_v, sems.at[0])
+    load.start()
     lane = lax.broadcasted_iota(jnp.int32, (8, OWN, LANES), 2)
     scale = 1.0 / 128.0
 
@@ -150,71 +179,96 @@
 
     lax.fori_loop(0, 16, convolve, 0)
 
-    for ch in range(OWN):
-        own = pl.ds(ch, ROWS, stride=OWN)
-        pair = jnp.concatenate([gated_s[own, :], grad_s[own, :]], axis=1).astype(BF16)
-        part = dot(first[...], jnp.concatenate([pair, pair], axis=0))
-        lhs = jnp.concatenate(
-            [turned(part[:, 128 * i : 128 * i + 128], tr[...], ti[...]) for i in range(2)], axis=0
-        )
-        spec = dot(wide(lhs), last[...])
-        gr, gi = spec[:128, :128], spec[:128, 128:]
-        dr, di = spec[128:, :128], spec[128:, 128:]
-        fr, fi = filt[ch][:, :128], filt[ch][:, 128:]
-        cross[ch] = jnp.concatenate([gr * dr + gi * di, gr * di - gi * dr], axis=1)
-        inner = jnp.concatenate([gr * fr - gi * fi, gr * fi + gi * fr], axis=1)
-        corr = jnp.concatenate([fr * dr + fi * di, fr * di - fi * dr], axis=1)
-        back = dot(wide(jnp.concatenate([inner, corr], axis=0)), last_back[...])
-        turn = jnp.concatenate(
-            [turned_back(back[128 * i : 128 * i + 128], tr[...], ti[...]) for i in range(2)], axis=1
-        )
-        y = dot(first_back[...], tall(turn))
-        inner_s[own, :] = y[:, :128]
-        corr_s[own, :] = y[:, 128:]
+    load.wait()
+    stores = []
+    for g in range(OWN // GROUP):
+        chans = range(GROUP * g, GROUP * g + GROUP)
+        lhs = []
+        for ch in chans:
+            own = pl.ds(ch, ROWS, stride=OWN)
+            pair = jnp.concatenate([gated_s[own, :], grad_s[own, :]], axis=1).astype(BF16)
+            part = dot(first[...], jnp.concatenate([pair, pair], axis=0))
+            lhs += [turned(part[:, 128 * i : 128 * i + 128], tr[...], ti[...]) for i in range(2)]
+        specs = dot(wide(jnp.concatenate(lhs, axis=0)), last[...])
+        lhs = []
+        for n, ch in enumerate(chans):
+            spec = specs[256 * n : 256 * n + 256]
+            gr, gi = spec[:128, :128], spec[:128, 128:]
+            dr, di = spec[128:, :128], spec[128:, 128:]
+            fr, fi = filt_v[ch][:, :128], filt_v[ch][:, 128:]
+            cross_v[ch] = jnp.concatenate([gr * dr + gi * di, gr * di - gi * dr], axis=1)
+            lhs.append(jnp.concatenate([gr * fr - gi * fi, gr * fi + gi * fr], axis=1))
+            lhs.append(jnp.concatenate([fr * dr + fi * di, fr * di - fi * dr], axis=1))
+        backs = dot(wide(jnp.concatenate(lhs, axis=0)), last_back[...])
+        for n, ch in enumerate(chans):
+            own = pl.ds(ch, ROWS, stride=OWN)
+            back = backs[256 * n : 256 * n + 256]
+            turn = jnp.concatenate(
+                [turned_back(back[128 * i : 128 * i + 128], tr[...], ti[...]) for i in range(2)], axis=1
+            )
+            y = dot(first_back[...], tall(turn))
+            inner_s[own, :] = y[:, :128]
+            corr_s[own, :] = y[:, 128:]
+        part = pl.ds(GROUP * g, GROUP)
+        stores.append(copy(cross_v.at[part], cross.at[part], sems.at[1 + g]))
+        stores[g].start()
 
     def finish(i, sums):
         at = pl.ds(8 * i, 8)
         flat = pl.ds(64 * i, 64)
         gated = gated_s[flat, :].reshape(8, OWN, LANES)
         grad = grad_s[flat, :].reshape(8, OWN, LANES)
-        inner = rounded(inner_s[flat, :].reshape(8, OWN, LANES) + skip[...] * gated)
-        dgated = rounded(corr_s[flat, :].reshape(8, OWN, LANES) + skip[...] * grad)
+        inner = rounded(inner_s[flat, :].reshape(8, OWN, LANES) + w[9] * gated)
+        dgated = rounded(corr_s[flat, :].reshape(8, OWN, LANES) + w[9] * grad)
         dconv = (rounded(cot_s[at] * inner), dgated * conv_s[1, at], dgated * conv_s[0, at])
         terms = [dconv[s] * raw_s[3 * s + j, at] for s in range(3) for j in range(3)]
         terms.append(grad * gated)
         sums = tuple(total + jnp.sum(term, axis=0) for total, term in zip(sums, terms))
+        firsts = []
         for value, off in ((dgated, 0), (inner, 256)):
             value = value.reshape(4, 2, OWN, LANES)
+            firsts.append(value[:, 0])
             both = jnp.concatenate([value[:, 0], value[:, 1]], axis=2)
-            out[pl.ds(4 * i, 4), :, off : off + 256] = both.astype(BF16)
+            for u in range(4):
+                at = pl.ds(512 * u + off, 256)
+                out_v[pl.ds(4 * i, 4), :, at] = both[:, 2 * u : 2 * u + 2].astype(BF16)
+        edge_s[pl.ds(4 * i, 4)] = jnp.where(lane[:4] < 2, firsts[0], pltpu.roll(firsts[1], 2, axis=2))
         return sums
 
     zero = jnp.zeros((OWN, LANES), F32)
-    sums = lax.fori_loop(0, 16, finish, (zero,) * 10)
+    edge_s[64] = zero
+    sums = (zero,) * 10
+    for g in range(4):
+        sums = lax.fori_loop(4 * g, 4 * g + 4, finish, sums)
+        part = (pl.ds(16 * g, 16), slice(None), pl.ds(0, TAIL))
+        stores.append(copy(out_v.at[part], out.at[part], sems.at[9 + g]))
+        stores[-1].start()
     totals = [jnp.sum(total, axis=1, keepdims=True) * scale for total in sums]
     dskip[...] = jnp.broadcast_to(totals[9], (OWN, LANES))
 
     spot = lax.broadcasted_iota(jnp.int32, (OWN, LANES), 1)
+    pairs = lax.broadcasted_iota(jnp.int32, (OWN, LANES), 0) // 2
+    spot = spot - 32 * pairs
     shared = zero
     for n in range(9):
         value = jnp.broadcast_to(totals[n], (OWN, LANES))
         high = rounded(value)
         mid = rounded(value - high)
-        for base, piece in ((0, high), (16, mid), (32, value - high - mid)):
+        for base, piece in ((0, high), (9, mid), (18, value - high - mid)):
             shared = jnp.where(spot == base + n, piece, shared)
     for g in range(4):
-        s0 = 16 * g
-        edge = []
-        for off, by in ((0, 48), (256, 50)):
-            if g < 3:
-                after = out[s0 : s0 + 32, :, off : off + 128].astype(F32)[1:17]
-            else:
-                after = out[s0 : s0 + 16, :, off : off + 128].astype(F32)
-                after = jnp.concatenate([after[1:], jnp.zeros((1, OWN, LANES), F32)], axis=0)
-            edge.append(pltpu.roll(after, by, axis=2))
-        rest = jnp.where(spot < 50, edge[0], edge[1])
-        extra = jnp.where(spot < 48, shared, jnp.where(spot < 52, rest, 0.0))
-        out[s0 : s0 + 16, :, 512:640] = extra.astype(BF16)
+        after = edge_s[pl.ds(16 * g + 1, 16)]
+        extra = jnp.broadcast_to(shared[None], (16, OWN, LANES))
+        for u in range(4):
+            here = (pairs == u) & (spot >= 27) & (spot < 31)
+            extra = jnp.where(here[None], pltpu.roll(after, 27 + 32 * u, axis=2), extra)
+        extra = extra[:, 0:2] + extra[:, 2:4] + extra[:, 4:6] + extra[:, 6:8]
+        out_v[16 * g : 16 * g + 16, :, TAIL:] = extra.astype(BF16)
+    part = (slice(None), slice(None), pl.ds(TAIL, LANES))
+    stores.append(copy(out_v.at[part], out.at[part], sems.at[13]))
+    stores[-1].start()
+    for store in stores:
+        store.wait()
 
 
 def cross_kernel(cross, tr, ti, last_back, first_back, out, rows):
@@ -231,21 +285,26 @@
         out[:, 128 * a : 128 * a + 128] = rows[8 * a : 8 * a + 8, :]
 
 
-def token_kernel(got, q, k, v, c, prev, nxt, w, mixed, dq, dk, dv, dshort):
+def token_kernel(
+    got, q, k, v, c, prev, nxt, w, mixed, dq, dk, dv, dshort
+):
     for j in range(4):
         cols = slice(128 * j, 128 * j + 128)
         own = slice(16 * j, 16 * j + 16)
 
-        def columns(off, width):
-            return got[own, :, off : off + width].astype(F32).reshape(128, width).T
-
-        dgated = columns(0, 256)
-        inner = columns(256, 256)
-        extra = columns(512, 128)
+        def columns(off):
+            parts = [got[own, :, 512 * u + off : 512 * u + off + 256] for u in range(4)]
+            return jnp.concatenate([p.astype(F32) for p in parts], axis=1).reshape(128, 256).T
+
+        dgated = columns(0)
+        inner = columns(256)
+        rest = got[own, :, TAIL : TAIL + 128].astype(F32)
+        parts = [rest if u == 0 else pltpu.roll(rest, 128 - 32 * u, axis=2) for u in range(4)]
+        extra = jnp.concatenate(parts, axis=1).reshape(128, 128).T
         for s in range(3):
             for n in range(3):
                 at = 3 * s + n
-                total = extra[at : at + 1] + extra[16 + at : 17 + at] + extra[32 + at : 33 + at]
+                total = extra[at : at + 1] + extra[9 + at : 10 + at] + extra[18 + at : 19 + at]
                 dshort[s, n : n + 1, cols] = total
         weight = [[w[s, n : n + 1, cols] for n in range(3)] for s in range(3)]
         cot = c[:, cols].astype(F32)
@@ -266,21 +325,23 @@
         q_ext = jnp.concatenate([prev[0:2, cols], q[:, cols].astype(F32)], axis=0)
         query = rounded(conv(q_ext, 0))
         mixed[:, cols] = (query * inner).astype(BF16)
-        dconv = jnp.concatenate([rounded(cot * inner), rounded(cot_n * extra[50:52])], axis=0)
+        dconv = jnp.concatenate([rounded(cot * inner), rounded(cot_n * extra[29:31])], axis=0)
         dq[:, cols] = back(dconv, 0)
-        dgated_ext = jnp.concatenate([dgated, extra[48:50]], axis=0)
+        dgated_ext = jnp.concatenate([dgated, extra[27:29]], axis=0)
         k_ext = jnp.concatenate([prev[2:4, cols], k[:, cols].astype(F32), nxt[0:2, cols]], axis=0)
         v_ext = jnp.concatenate([prev[4:6, cols], v[:, cols].astype(F32), nxt[2:4, cols]], axis=0)
         dk[:, cols] = back(dgated_ext * conv(v_ext, 2), 1)
         dv[:, cols] = back(dgated_ext * conv(k_ext, 1), 2)
 
 
-def call(kernel, outs, scratch=(), flops=0, moved=0, limit=24):
-    one = not isinstance(outs, list)
-    shapes = [outs] if one else outs
+def call(kernel, outs, ins, scratch=(), flops=0, moved=0, limit=24):
+    shapes, specs = [o[0] for o in outs], [o[1] for o in outs]
+    one = len(outs) == 1
     return pl.pallas_call(
         kernel,
         out_shape=shapes[0] if one else shapes,
+        in_specs=list(ins),
+        out_specs=specs[0] if one else specs,
         scratch_shapes=list(scratch),
         compiler_params=pltpu.CompilerParams(vmem_limit_bytes=limit << 20),
         cost_estimate=pl.CostEstimate(flops=flops, bytes_accessed=moved, transcendentals=0),
@@ -291,49 +352,66 @@
     return jax.ShapeDtypeStruct(dims, kind)
 
 
+def pack():
+    packed = shape(64, 16, 512, kind=BF16)
+    stream = VMEM((256, 512), BF16)
+    return call(
+        pack_kernel, [(packed, HBM)], [HBM] * 4,
+        [stream] * 4 + [VMEM((64, 16, 512), BF16), pltpu.SemaphoreType.DMA((8,))],
+        moved=2 << 20, limit=60,
+    )
+
+
+def channels():
+    big = VMEM((128, OWN, LANES), F32)
+    flat = VMEM((1024, LANES), F32)
+    spectra = VMEM((OWN, 128, 256), F32)
+    return call(
+        channel_kernel,
+        [(shape(64, 2, TAIL + 128, kind=BF16), HBM), (shape(SPARE, 128, 256), HBM), (shape(OWN, LANES), WHOLE)],
+        [WHOLE] * 2 + [HBM] + [WHOLE] * 6,
+        [flat, flat, flat, flat, big, VMEM((2, 128, OWN, LANES), F32), VMEM((9, 128, OWN, LANES), F32),
+         VMEM((65, OWN, LANES), F32), spectra, spectra, VMEM((64, 2, TAIL + 128), BF16),
+         pltpu.SemaphoreType.DMA((14,))],
+        flops=4 * 10**9, moved=4 << 20, limit=50,
+    )
+
+
 def body(query_in, key_in, value_in, short_weights, long_filter, skip_gain, cotangent):
     t = tables()
     turns = (t["turn_re"], t["turn_im"])
     count = lax.axis_size("ctx")
-    here = lax.axis_index("ctx")
-
-    packed = call(pack_kernel, shape(64, 16, 512, kind=BF16), moved=2 << 20)(
-        query_in, key_in, value_in, cotangent
-    )
+
+    tokens = shape(256, 512, kind=BF16)
+    flat = VMEM((1024, LANES), F32)
+    packed = pack()(query_in, key_in, value_in, cotangent)
     seqs = lax.all_to_all(packed, "ctx", split_axis=0, concat_axis=0, tiled=True)
 
-    spectrum = call(
-        filter_kernel, shape(OWN, 128, 256), [VMEM((1024, LANES), F32)],
-        flops=10**9, moved=2 << 20,
-    )(long_filter, t["first_three"], *turns, t["last"])
+    here = lax.axis_index("ctx").astype(jnp.int32).reshape(1)
+    spectrum, own_w = call(
+        filter_kernel,
+        [(shape(SPARE, 128, 256), WHOLE), (shape(10, OWN, LANES), WHOLE)],
+        [pl.BlockSpec(memory_space=pltpu.SMEM)] + [WHOLE] * 7, [flat],
+        flops=10**9, moved=2 << 20, limit=60,
+    )(here, long_filter, short_weights, skip_gain[:, None], t["first_three"], *turns, t["last"])
 
     ends = jnp.concatenate([query_in[254:], key_in[254:], value_in[254:]], axis=0)
     starts = jnp.concatenate([key_in[:2], value_in[:2], cotangent[:2]], axis=0)
     prev = lax.ppermute(ends, "ctx", [(i, i + 1) for i in range(count - 1)]).astype(F32)
     nxt = lax.ppermute(starts, "ctx", [(i + 1, i) for i in range(count - 1)]).astype(F32)
 
-    own_w = lax.dynamic_slice_in_dim(short_weights, OWN * here, OWN, axis=2).reshape(9, OWN, 1)
-    own_w = jnp.broadcast_to(own_w, (9, OWN, LANES))
-    own_skip = jnp.broadcast_to(skip_gain[:, None], (OWN, LANES))
-
-    big = VMEM((128, OWN, LANES), F32)
-    flat = VMEM((1024, LANES), F32)
-    answer, cross, dskip = call(
-        channel_kernel,
-        [shape(64, OWN, 640, kind=BF16), shape(OWN, 128, 256), shape(OWN, LANES)],
-        [flat, flat, flat, flat, big, VMEM((2, 128, OWN, LANES), F32), VMEM((9, 128, OWN, LANES), F32)],
-        flops=4 * 10**9, moved=4 << 20,
-    )(seqs, own_w, own_skip, spectrum, t["first_pair"], *turns, t["last"], t["last_back"], t["first_back"])
+    answer, cross, dskip = channels()(
+        seqs, own_w, spectrum, t["first_pair"], *turns, t["last"], t["last_back"], t["first_back"]
+    )
 
     got = lax.all_to_all(answer, "ctx", split_axis=0, concat_axis=0, tiled=True)
 
     d_filter = call(
-        cross_kernel, shape(OWN, 16384), [flat], flops=10**9, moved=2 << 20
+        cross_kernel, [(shape(OWN, 16384), WHOLE)], [WHOLE] * 5, [flat], flops=10**9, moved=2 << 20, limit=60
     )(cross, *turns, t["last_back"], t["first_back"])
 
-    tokens = shape(256, 512, kind=BF16)
     mixed, d_query, d_key, d_value, d_short = call(
-        token_kernel, [tokens, tokens, tokens, tokens, shape(3, 3, 512)], moved=3 << 20
+        token_kernel, [(tokens, WHOLE)] * 4 + [(shape(3, 3, 512), WHOLE)], [WHOLE] * 8, moved=3 << 20
     )(got, query_in, key_in, value_in, cotangent, prev, nxt, short_weights)
     return (mixed, d_query, d_key, d_value, d_filter, dskip[:, 0], d_short)
 

time: 137 us -> 128 us (0.934)
  local copies, waits for them, and re-layouts: 9.81 us -> 2.16 us
  waiting for transfers between devices: 78.3 us -> 71.5 us
  Pallas kernels: 17.3 us -> 22.9 us
    unnamed x44 -> x26, local copies, waits for them, and re-layouts: 8.26 us -> 0.84 us
    pallas_call x5, Pallas kernels: 17.3 us -> 22.9 us  [the longest x1 8.31 us: body(): channels()]
    ppermute x1, waiting for transfers between devices: 17.2 us -> 13.7 us  [body(): lax.ppermute(ends, 'ctx', [(i, i + 1) for i in range(count - 1)])]
    all_to_all x1, waiting for transfers between devices: 51.3 us -> 48.8 us  [body(): lax.all_to_all(packed, 'ctx', split_axis=0, concat_axis=0, tiled=True)]
  transfers between devices with their start and end apart: 4 -> 4, of which waited for: 4 -> 4; matrix products, arithmetic and copies ran while one was open for 1% -> 1% of each run, Pallas kernels for 3% -> 7%
where the time goes in v2:
time: 128 us
  waiting for transfers between devices  71.5 us (56%)
  starting transfers between devices  30.4 us (24%)
  Pallas kernels  22.9 us (18%)
  local copies, waits for them, and re-layouts  2.16 us (2%)
    all_to_all x1, waiting for transfers between devices, body(): lax.all_to_all(packed, 'ctx', split_axis=0, concat_axis=0, tiled=True)  48.8 us
    all_to_all x1, starting transfers between devices, body(): lax.all_to_all(packed, 'ctx', split_axis=0, concat_axis=0, tiled=True)  18.7 us
    ppermute x1, waiting for transfers between devices, body(): lax.ppermute(ends, 'ctx', [(i, i + 1) for i in range(count - 1)])  13.7 us
    pallas_call x1, Pallas kernels, body(): channels()  8.31 us
    all_to_all x1, starting transfers between devices, body(): got = lax.all_to_all(answer, 'ctx', split_axis=0, concat_axis=0, tiled=True)  6.92 us
    ppermute x1, waiting for transfers between devices, body(): lax.ppermute(starts, 'ctx', [(i + 1, i) for i in range(count - 1)])  5.24 us
    pallas_call x1, Pallas kernels, body(): call(cross_kernel, [(shape(OWN, 16384), WHOLE)], [WHOLE] * 5, [flat], flo...  4.8 us
    pallas_call x1, Pallas kernels, body(): call(filter_kernel, [(shape(SPARE, 128, 256), WHOLE), (shape(10, OWN, LAN...  4.37 us
  transfers between devices with their start and end apart: 4, of which 4 were waited for; matrix products, arithmetic and copies ran while one was open for 1% of the time, Pallas kernels for 7%

profile of v2, /device:TPU:24, one launch (start us, length us, event | category | flops | bytes accessed | tf_op | source)
XLA Modules:
  0.0 127.8 jit_solution(16286515390726940476)
XLA Ops:
  0.6 0.0 copy-start.12
  0.6 2.4 %shard_map.189 = bf16[64,16,512]{2,1,0:T(8,128)(2,1)} custom-call(bf16[256,512]{1,0:T(8,128)(2,1)} %q.3, bf16[256,512]{1,0:T(8,128)(2,1)} %k.3, bf16[256,512]{1,0:T(8,128)(2,1)} %v.3, bf16[256,512]{1,0:T(8,128)(2,1)} %c.3), custom_call_target="tpu_custom_call" | custom-call | bytes 2097152 | tf_op jit(solution)/shard_map/pallas_call | solution.py:387
  3.0 0.0 copy-start.4
  3.0 0.0 copy-start.5
  3.0 0.0 copy-start.6
  3.1 0.0 copy-start.7
  3.1 0.0 copy-start.9
  3.1 0.0 copy-start.10
  3.1 18.7 %all-to-all-start = ((bf16[64,16,512]{2,1,0:T(8,128)(2,1)}), bf16[64,16,512]{2,1,0:T(8,128)(2,1)S(1)}, u32[]{:S(2)}, u32[]{:S(2)}) async-start(bf16[64,16,512]{2,1,0:T(8,128)(2,1)} %shard_map.189), calls=%async_computation | async-start | bytes 2097152 | tf_op jit(solution)/shard_map/all_to_all | solution.py:388
  21.8 0.0 copy-done.12
  21.8 0.7 copy.22.skip
  22.5 4.4 %shard_map.190 = (f32[24,128,256]{2,1,0:T(8,128)}, f32[10,8,128]{2,1,0:T(8,128)}) custom-call(s32[1]{0:T(128)} %bitcast.here, f32[8,16384]{1,0:T(8,128)} %f.1, f32[3,3,512]{2,1,0:T(4,128)} %w.3, f32[8,1]{1,0:T(8,128)} %copy.22.skip, bf16[256,384]{1,0:T(8,128)(2,1)} %constant.20.clone.first, f32[128,128]{1,0:T(8,128)} %constant.21.clone.tr, ...), custom_call_target="tpu_custom_call" | custom-call | flops 1000000000 | bytes 2097152 | tf_op jit(solution)/shard_map/pallas_call | solution.py:391
  26.9 48.8 %all-to-all-done.x = bf16[64,16,512]{2,1,0:T(8,128)(2,1)S(1)} async-done(((bf16[64,16,512]{2,1,0:T(8,128)(2,1)}), bf16[64,16,512]{2,1,0:T(8,128)(2,1)S(1)}, u32[]{:S(2)}, u32[]{:S(2)}) %all-to-all-start) | async-done | bytes 1048608 | tf_op jit(solution)/shard_map/all_to_all | solution.py:388
  75.7 0.0 copy-done.4
  75.7 0.0 copy-done.5
  75.7 0.0 copy-done.6
  75.7 0.0 copy-done.7
  75.7 0.0 copy-done.9
  75.7 0.0 copy-start.11
  75.7 0.8 copy-done.11
  76.5 8.3 %shard_map.191 = (bf16[64,2,2176]{2,1,0:T(2,128)(2,1)}, f32[24,128,256]{2,1,0:T(8,128)}, f32[8,128]{1,0:T(8,128)S(1)}) custom-call(bf16[64,16,512]{2,1,0:T(8,128)(2,1)S(1)} %all-to-all-done.x, f32[10,8,128]{2,1,0:T(8,128)S(1)} %copy-done.11, f32[24,128,256]{2,1,0:T(8,128)} %get-tuple-element.18.filt, bf16[256,256]{1,0:T(8,128)(2,1)S(1)} %copy-done.10, ...), custom_call_target="tpu_custom_call" | custom-call | flops 4000000000 | bytes 4194304 | tf_op jit(solution)/shard_map/pallas_call | solution.py:403
  84.8 0.0 copy-start.3
  84.8 0.0 copy-start.8
  84.8 6.9 %all-to-all-start.1 = ((bf16[64,2,2176]{2,1,0:T(2,128)(2,1)}), bf16[64,2,2176]{2,1,0:T(2,128)(2,1)S(1)}, u32[]{:S(2)}, u32[]{:S(2)}) async-start(bf16[64,2,2176]{2,1,0:T(2,128)(2,1)} %get-tuple-element.19), calls=%async_computation.1 | async-start | bytes 1114112 | tf_op jit(solution)/shard_map/all_to_all | solution.py:407
  91.8 3.5 %collective-permute-start = (bf16[6,512]{1,0:T(8,128)(2,1)S(1)}, bf16[6,512]{1,0:T(8,128)(2,1)S(1)}, u32[]{:S(2)}, u32[]{:S(2)}) collective-permute-start(bf16[6,512]{1,0:T(8,128)(2,1)S(1)} %pad_maximum_fusion), channel_id=1, source_target_pairs={{0,8},{8,16},{16,24},{24,32},{32,40},{40,48},{48,56},{56,64},{64,7... | collective-permute-start | bytes 18440 | tf_op jit(solution)/shard_map/ppermute | solution.py:400
  95.4 1.3 %collective-permute-start.1 = (bf16[6,512]{1,0:T(8,128)(2,1)S(1)}, bf16[6,512]{1,0:T(8,128)(2,1)S(1)}, u32[]{:S(2)}, u32[]{:S(2)}) collective-permute-start(bf16[6,512]{1,0:T(8,128)(2,1)S(1)} %pad_maximum_fusion.1), channel_id=1, source_target_pairs={{8,0},{16,8},{24,16},{32,24},{40,32},{48,40},{56,48},{64,56},{72,6... | collective-permute-start | bytes 18440 | tf_op jit(solution)/shard_map/ppermute | solution.py:401
  96.7 13.7 %collective-permute-done = bf16[6,512]{1,0:T(8,128)(2,1)S(1)} collective-permute-done((bf16[6,512]{1,0:T(8,128)(2,1)S(1)}, bf16[6,512]{1,0:T(8,128)(2,1)S(1)}, u32[]{:S(2)}, u32[]{:S(2)}) %collective-permute-start) | collective-permute-done | bytes 6176 | tf_op jit(solution)/shard_map/ppermute | solution.py:400
  110.3 5.2 %collective-permute-done.1 = bf16[6,512]{1,0:T(8,128)(2,1)S(1)} collective-permute-done((bf16[6,512]{1,0:T(8,128)(2,1)S(1)}, bf16[6,512]{1,0:T(8,128)(2,1)S(1)}, u32[]{:S(2)}, u32[]{:S(2)}) %collective-permute-start.1) | collective-permute-done | bytes 6176 | tf_op jit(solution)/shard_map/ppermute | solution.py:401
  115.6 4.8 %shard_map.193 = f32[8,16384]{1,0:T(8,128)} custom-call(f32[24,128,256]{2,1,0:T(8,128)} %get-tuple-element.24.cross, f32[128,128]{1,0:T(8,128)} %constant.21.clone.tr, f32[128,128]{1,0:T(8,128)} %constant.22.clone.ti, bf16[768,256]{1,0:T(8,128)(2,1)} %constant.25.clone.last_back, bf16[128,768]{1,0:T(8,128)(2,1)} %constant.26.clone.first_back), custom_call_target="tpu_custom_call" | custom-call | flops 1000000000 | bytes 2097152 | tf_op jit(solution)/shard_map/pallas_call | solution.py:409
  120.4 0.6 slice_reduce_fusion
  121.0 3.8 %all-to-all-done.1.got = bf16[64,2,2176]{2,1,0:T(2,128)(2,1)S(1)} async-done(((bf16[64,2,2176]{2,1,0:T(2,128)(2,1)}), bf16[64,2,2176]{2,1,0:T(2,128)(2,1)S(1)}, u32[]{:S(2)}, u32[]{:S(2)}) %all-to-all-start.1) | async-done | bytes 557088 | tf_op jit(solution)/shard_map/all_to_all | solution.py:407
  124.8 3.1 %shard_map.192 = (bf16[256,512]{1,0:T(8,128)(2,1)}, bf16[256,512]{1,0:T(8,128)(2,1)}, bf16[256,512]{1,0:T(8,128)(2,1)}, bf16[256,512]{1,0:T(8,128)(2,1)}, f32[3,3,512]{2,1,0:T(4,128)}) custom-call(bf16[64,2,2176]{2,1,0:T(2,128)(2,1)S(1)} %all-to-all-done.1.got, bf16[256,512]{1,0:T(8,128)(2,1)S(1)} %copy-done.2, bf16[256,512]{1,0:T(8,128)(2,1)S(1)} %copy-done, ...), custom_call_target="tpu_custom_call" | custom-call | bytes 3145728 | tf_op jit(solution)/shard_map/pallas_call | solution.py:413
  (17 shorter events, 0.1 us)
Async XLA Ops:
  0.6 21.2 %copy-start.12 = (f32[8]{0:T(128)S(1)}, f32[8]{0:T(128)}, u32[]{:S(2)}) copy-start(f32[8]{0:T(128)} %param.19) | copy-start | bytes 100
  3.0 72.6 %copy-start.4 = (bf16[768,256]{1,0:T(8,128)(2,1)S(1)}, bf16[768,256]{1,0:T(8,128)(2,1)}, u32[]{:S(2)}) copy-start(bf16[768,256]{1,0:T(8,128)(2,1)} %constant.25.clone.last_back) | copy-start | bytes 1179652
  3.0 72.6 %copy-start.5 = (bf16[128,768]{1,0:T(8,128)(2,1)S(1)}, bf16[128,768]{1,0:T(8,128)(2,1)}, u32[]{:S(2)}) copy-start(bf16[128,768]{1,0:T(8,128)(2,1)} %constant.26.clone.first_back) | copy-start | bytes 589828
  3.0 72.6 %copy-start.6 = (f32[128,128]{1,0:T(8,128)S(1)}, f32[128,128]{1,0:T(8,128)}, u32[]{:S(2)}) copy-start(f32[128,128]{1,0:T(8,128)} %constant.21.clone.tr) | copy-start | bytes 196612
  3.1 72.6 %copy-start.7 = (f32[128,128]{1,0:T(8,128)S(1)}, f32[128,128]{1,0:T(8,128)}, u32[]{:S(2)}) copy-start(f32[128,128]{1,0:T(8,128)} %constant.22.clone.ti) | copy-start | bytes 196612
  3.1 72.6 %copy-start.9 = (bf16[768,256]{1,0:T(8,128)(2,1)S(1)}, bf16[768,256]{1,0:T(8,128)(2,1)}, u32[]{:S(2)}) copy-start(bf16[768,256]{1,0:T(8,128)(2,1)} %constant.23.clone.last) | copy-start | bytes 1179652
  3.1 72.6 %copy-start.10 = (bf16[256,256]{1,0:T(8,128)(2,1)S(1)}, bf16[256,256]{1,0:T(8,128)(2,1)}, u32[]{:S(2)}) copy-start(bf16[256,256]{1,0:T(8,128)(2,1)} %constant.24.clone.first) | copy-start | bytes 393220
  3.1 72.6 %all-to-all-start = ((bf16[64,16,512]{2,1,0:T(8,128)(2,1)}), bf16[64,16,512]{2,1,0:T(8,128)(2,1)S(1)}, u32[]{:S(2)}, u32[]{:S(2)}) async-start(bf16[64,16,512]{2,1,0:T(8,128)(2,1)} %shard_map.189), calls=%async_computation | async-start | bytes 2097152 | tf_op jit(solution)/shard_map/all_to_all | solution.py:388
  75.7 0.8 copy-start.11
  76.5 15.3 %copy-start.2 = (bf16[256,512]{1,0:T(8,128)(2,1)S(1)}, bf16[256,512]{1,0:T(8,128)(2,1)}, u32[]{:S(2)}) copy-start(bf16[256,512]{1,0:T(8,128)(2,1)} %q.3) | copy-start | bytes 786436
  76.5 15.3 %copy-start = (bf16[256,512]{1,0:T(8,128)(2,1)S(1)}, bf16[256,512]{1,0:T(8,128)(2,1)}, u32[]{:S(2)}) copy-start(bf16[256,512]{1,0:T(8,128)(2,1)} %k.3) | copy-start | bytes 786436
  76.5 15.3 %copy-start.1 = (bf16[256,512]{1,0:T(8,128)(2,1)S(1)}, bf16[256,512]{1,0:T(8,128)(2,1)}, u32[]{:S(2)}) copy-start(bf16[256,512]{1,0:T(8,128)(2,1)} %v.3) | copy-start | bytes 786436
  76.5 18.8 %slice-start = ((bf16[256,512]{1,0:T(8,128)(2,1)}), bf16[2,512]{1,0:T(2,128)(2,1)S(1)}, s32[]{:S(2)}) async-start(bf16[256,512]{1,0:T(8,128)(2,1)} %c.3), calls=%async_computation.2 | async-start | bytes 4096 | tf_op jit(solution)/shard_map/slice | solution.py:399
  84.8 40.0 %copy-start.3 = (bf16[256,512]{1,0:T(8,128)(2,1)S(1)}, bf16[256,512]{1,0:T(8,128)(2,1)}, u32[]{:S(2)}) copy-start(bf16[256,512]{1,0:T(8,128)(2,1)} %c.3) | copy-start | bytes 786436
  84.8 39.9 %copy-start.8 = (f32[3,3,512]{2,1,0:T(4,128)S(1)}, f32[3,3,512]{2,1,0:T(4,128)}, u32[]{:S(2)}) copy-start(f32[3,3,512]{2,1,0:T(4,128)} %w.3) | copy-start | bytes 55300
  84.8 39.9 %all-to-all-start.1 = ((bf16[64,2,2176]{2,1,0:T(2,128)(2,1)}), bf16[64,2,2176]{2,1,0:T(2,128)(2,1)S(1)}, u32[]{:S(2)}, u32[]{:S(2)}) async-start(bf16[64,2,2176]{2,1,0:T(2,128)(2,1)} %get-tuple-element.19), calls=%async_computation.1 | async-start | bytes 1114112 | tf_op jit(solution)/shard_map/all_to_all | solution.py:407
  91.8 18.5 %collective-permute-start = (bf16[6,512]{1,0:T(8,128)(2,1)S(1)}, bf16[6,512]{1,0:T(8,128)(2,1)S(1)}, u32[]{:S(2)}, u32[]{:S(2)}) collective-permute-start(bf16[6,512]{1,0:T(8,128)(2,1)S(1)} %pad_maximum_fusion), channel_id=1, source_target_pairs={{0,8},{8,16},{16,24},{24,32},{32,40},{40,48},{48,56},{56,64},{64,7... | collective-permute-start | bytes 18440 | tf_op jit(solution)/shard_map/ppermute | solution.py:400
  95.4 20.2 %collective-permute-start.1 = (bf16[6,512]{1,0:T(8,128)(2,1)S(1)}, bf16[6,512]{1,0:T(8,128)(2,1)S(1)}, u32[]{:S(2)}, u32[]{:S(2)}) collective-permute-start(bf16[6,512]{1,0:T(8,128)(2,1)S(1)} %pad_maximum_fusion.1), channel_id=1, source_target_pairs={{8,0},{16,8},{24,16},{32,24},{40,32},{48,40},{56,48},{64,56},{72,6... | collective-permute-start | bytes 18440 | tf_op jit(solution)/shard_map/ppermute | solution.py:401

commit v3 on v2

--- a/solution.py
+++ b/solution.py
@@ -16,7 +16,7 @@
 VMEM = pltpu.VMEM
 HBM = pl.BlockSpec(memory_space=pltpu.HBM)
 WHOLE = pl.BlockSpec(memory_space=pltpu.VMEM)
-GROUP = 4
+GROUP = 8
 SPARE = 24
 TAIL = 2048
 
@@ -97,8 +97,8 @@
     for j in range(4):
         cols = slice(128 * j, 128 * j + 128)
         for top, low, off in ((k_v, q_v, 0), (v_v, c_v, 256)):
-            upper = top[:, cols].astype(F32).T.reshape(16, OWN, 256)
-            lower = low[:, cols].astype(F32).T.reshape(16, OWN, 256)
+            upper = top[:, cols].T.astype(F32).reshape(16, OWN, 256)
+            lower = low[:, cols].T.astype(F32).reshape(16, OWN, 256)
             both = jnp.concatenate([upper, lower], axis=1)
             out_v[16 * j : 16 * j + 16, :, off : off + 256] = both.astype(BF16)
         part = pl.ds(16 * j, 16)
@@ -108,7 +108,7 @@
         store.wait()
 
 
-def filter_kernel(here, f, w, skip, first, tr, ti, last, out, own_w, rows):
+def weight_kernel(here, w, skip, after, own_w):
     wanted = OWN * here[0] + lax.broadcasted_iota(jnp.int32, (OWN, 512), 0)
     mine = lax.broadcasted_iota(jnp.int32, (OWN, 512), 1) == wanted
     for s in range(3):
@@ -116,6 +116,9 @@
             value = jnp.sum(jnp.where(mine, w[s, n : n + 1, :], 0.0), axis=1, keepdims=True)
             own_w[3 * s + n] = jnp.broadcast_to(value, (OWN, LANES))
     own_w[9] = jnp.broadcast_to(skip[...], (OWN, LANES))
+
+
+def filter_kernel(f, first, tr, ti, last, out, rows):
     for a in range(ROWS):
         rows[8 * a : 8 * a + 8, :] = f[:, 128 * a : 128 * a + 128]
     for p in range(OWN // 2):
@@ -177,7 +180,7 @@
         grad_s[flat, :] = rounded(cot * rounded(convs[0])).reshape(64, LANES)
         return carry
 
-    lax.fori_loop(0, 16, convolve, 0)
+    lax.fori_loop(0, 16, convolve, 0, unroll=4)
 
     load.wait()
     stores = []
@@ -239,7 +242,7 @@
     edge_s[64] = zero
     sums = (zero,) * 10
     for g in range(4):
-        sums = lax.fori_loop(4 * g, 4 * g + 4, finish, sums)
+        sums = lax.fori_loop(4 * g, 4 * g + 4, finish, sums, unroll=4)
         part = (pl.ds(16 * g, 16), slice(None), pl.ds(0, TAIL))
         stores.append(copy(out_v.at[part], out.at[part], sems.at[9 + g]))
         stores[-1].start()
@@ -285,9 +288,22 @@
         out[:, 128 * a : 128 * a + 128] = rows[8 * a : 8 * a + 8, :]
 
 
-def token_kernel(
-    got, q, k, v, c, prev, nxt, w, mixed, dq, dk, dv, dshort
-):
+def conv_kernel(q, k, v, prev, nxt, w, query, ck, cv):
+    for j in range(4):
+        cols = slice(128 * j, 128 * j + 128)
+
+        def conv(parts, s):
+            seq = jnp.concatenate(parts, axis=0)
+            rows = seq.shape[0] - 2
+            tap = [w[s, n : n + 1, cols] for n in range(3)]
+            return tap[0] * seq[2:] + tap[1] * seq[1 : 1 + rows] + tap[2] * seq[:rows]
+
+        query[:, cols] = conv([prev[0:2, cols], q[:, cols].astype(F32)], 0).astype(BF16)
+        ck[0:258, cols] = conv([prev[2:4, cols], k[:, cols].astype(F32), nxt[0:2, cols]], 1)
+        cv[0:258, cols] = conv([prev[4:6, cols], v[:, cols].astype(F32), nxt[2:4, cols]], 2)
+
+
+def token_kernel(got, query, ck, cv, c, nxt, w, mixed, dq, dk, dv, dshort, stage):
     for j in range(4):
         cols = slice(128 * j, 128 * j + 128)
         own = slice(16 * j, 16 * j + 16)
@@ -296,8 +312,6 @@
             parts = [got[own, :, 512 * u + off : 512 * u + off + 256] for u in range(4)]
             return jnp.concatenate([p.astype(F32) for p in parts], axis=1).reshape(128, 256).T
 
-        dgated = columns(0)
-        inner = columns(256)
         rest = got[own, :, TAIL : TAIL + 128].astype(F32)
         parts = [rest if u == 0 else pltpu.roll(rest, 128 - 32 * u, axis=2) for u in range(4)]
         extra = jnp.concatenate(parts, axis=1).reshape(128, 128).T
@@ -306,32 +320,25 @@
                 at = 3 * s + n
                 total = extra[at : at + 1] + extra[9 + at : 10 + at] + extra[18 + at : 19 + at]
                 dshort[s, n : n + 1, cols] = total
-        weight = [[w[s, n : n + 1, cols] for n in range(3)] for s in range(3)]
-        cot = c[:, cols].astype(F32)
-        cot_n = nxt[4:6, cols]
-
-        def conv(seq, s):
-            rows = seq.shape[0] - 2
-            return (
-                weight[s][0] * seq[2:] + weight[s][1] * seq[1 : 1 + rows] + weight[s][2] * seq[:rows]
-            )
-
-        def back(seq, s):
-            total = (
-                weight[s][0] * seq[:256] + weight[s][1] * seq[1:257] + weight[s][2] * seq[2:258]
-            )
+
+        def back(s):
+            seq = stage.at[j, s]
+            tap = [w[s, n : n + 1, cols] for n in range(3)]
+            total = tap[0] * seq[0:256, :] + tap[1] * seq[1:257, :] + tap[2] * seq[2:258, :]
             return total.astype(BF16)
 
-        q_ext = jnp.concatenate([prev[0:2, cols], q[:, cols].astype(F32)], axis=0)
-        query = rounded(conv(q_ext, 0))
-        mixed[:, cols] = (query * inner).astype(BF16)
-        dconv = jnp.concatenate([rounded(cot * inner), rounded(cot_n * extra[29:31])], axis=0)
-        dq[:, cols] = back(dconv, 0)
-        dgated_ext = jnp.concatenate([dgated, extra[27:29]], axis=0)
-        k_ext = jnp.concatenate([prev[2:4, cols], k[:, cols].astype(F32), nxt[0:2, cols]], axis=0)
-        v_ext = jnp.concatenate([prev[4:6, cols], v[:, cols].astype(F32), nxt[2:4, cols]], axis=0)
-        dk[:, cols] = back(dgated_ext * conv(v_ext, 2), 1)
-        dv[:, cols] = back(dgated_ext * conv(k_ext, 1), 2)
+        inner = columns(256)
+        mixed[:, cols] = (query[:, cols].astype(F32) * inner).astype(BF16)
+        stage[j, 0, 0:256, :] = rounded(c[:, cols].astype(F32) * inner)
+        stage[j, 0, 256:258, :] = rounded(nxt[4:6, cols] * extra[29:31])
+        dq[:, cols] = back(0)
+        dgated = columns(0)
+        stage[j, 1, 0:256, :] = dgated * cv[0:256, cols]
+        stage[j, 1, 256:258, :] = extra[27:29] * cv[256:258, cols]
+        dk[:, cols] = back(1)
+        stage[j, 2, 0:256, :] = dgated * ck[0:256, cols]
+        stage[j, 2, 256:258, :] = extra[27:29] * ck[256:258, cols]
+        dv[:, cols] = back(2)
 
 
 def call(kernel, outs, ins, scratch=(), flops=0, moved=0, limit=24):
@@ -388,12 +395,14 @@
     seqs = lax.all_to_all(packed, "ctx", split_axis=0, concat_axis=0, tiled=True)
 
     here = lax.axis_index("ctx").astype(jnp.int32).reshape(1)
-    spectrum, own_w = call(
-        filter_kernel,
-        [(shape(SPARE, 128, 256), WHOLE), (shape(10, OWN, LANES), WHOLE)],
-        [pl.BlockSpec(memory_space=pltpu.SMEM)] + [WHOLE] * 7, [flat],
+    spectrum = call(
+        filter_kernel, [(shape(SPARE, 128, 256), WHOLE)], [WHOLE] * 5, [flat],
         flops=10**9, moved=2 << 20, limit=60,
-    )(here, long_filter, short_weights, skip_gain[:, None], t["first_three"], *turns, t["last"])
+    )(long_filter, t["first_three"], *turns, t["last"])
+    own_w = call(
+        weight_kernel, [(shape(10, OWN, LANES), WHOLE)],
+        [pl.BlockSpec(memory_space=pltpu.SMEM), WHOLE, WHOLE, HBM], moved=1 << 20,
+    )(here, short_weights, skip_gain[:, None], spectrum)
 
     ends = jnp.concatenate([query_in[254:], key_in[254:], value_in[254:]], axis=0)
     starts = jnp.concatenate([key_in[:2], value_in[:2], cotangent[:2]], axis=0)
@@ -410,9 +419,14 @@
         cross_kernel, [(shape(OWN, 16384), WHOLE)], [WHOLE] * 5, [flat], flops=10**9, moved=2 << 20, limit=60
     )(cross, *turns, t["last_back"], t["first_back"])
 
+    extended = shape(264, 512)
+    query, conv_k, conv_v = call(
+        conv_kernel, [(tokens, WHOLE), (extended, WHOLE), (extended, WHOLE)], [WHOLE] * 6, moved=2 << 20
+    )(query_in, key_in, value_in, prev, nxt, short_weights)
     mixed, d_query, d_key, d_value, d_short = call(
-        token_kernel, [(tokens, WHOLE)] * 4 + [(shape(3, 3, 512), WHOLE)], [WHOLE] * 8, moved=3 << 20
-    )(got, query_in, key_in, value_in, cotangent, prev, nxt, short_weights)
+        token_kernel, [(tokens, WHOLE)] * 4 + [(shape(3, 3, 512), WHOLE)], [WHOLE] * 7,
+        [VMEM((4, 3, 264, LANES), F32)], moved=3 << 20,
+    )(got, query, conv_k, conv_v, cotangent, nxt, short_weights)
     return (mixed, d_query, d_key, d_value, d_filter, dskip[:, 0], d_short)
 
 

time: 128 us -> 125 us (0.977)
  waiting for transfers between devices: 71.5 us -> 69.1 us
  Pallas kernels: 22.9 us -> 21.6 us
    all_to_all x1, waiting for transfers between devices: 48.8 us -> 47.3 us  [body(): lax.all_to_all(packed, 'ctx', split_axis=0, concat_axis=0, tiled=True)]
    pallas_call x1 -> x3, Pallas kernels: 4.37 us -> 5.29 us  [the longest x1 4.43 us: body(): call(filter_kernel, [(shape(SPARE, 128, 256), WHOLE)], [WHOLE] * 5, [flat...]
  transfers between devices with their start and end apart: 4 -> 4, of which waited for: 4 -> 4; matrix products, arithmetic and copies ran while one was open for 1% -> 1% of each run, Pallas kernels for 7% -> 8%
where the time goes in v3:
time: 125 us
  waiting for transfers between devices  69.1 us (55%)
  starting transfers between devices  30.3 us (24%)
  Pallas kernels  21.6 us (17%)
  local copies, waits for them, and re-layouts  2.69 us (2%)
    all_to_all x1, waiting for transfers between devices, body(): lax.all_to_all(packed, 'ctx', split_axis=0, concat_axis=0, tiled=True)  47.3 us
    all_to_all x1, starting transfers between devices, body(): lax.all_to_all(packed, 'ctx', split_axis=0, concat_axis=0, tiled=True)  18.6 us
    ppermute x1, waiting for transfers between devices, body(): lax.ppermute(ends, 'ctx', [(i, i + 1) for i in range(count - 1)])  13.7 us
    pallas_call x1, Pallas kernels, body(): channels()  7.04 us
    all_to_all x1, starting transfers between devices, body(): got = lax.all_to_all(answer, 'ctx', split_axis=0, concat_axis=0, tiled=True)  6.93 us
    ppermute x1, waiting for transfers between devices, body(): lax.ppermute(starts, 'ctx', [(i + 1, i) for i in range(count - 1)])  5.24 us
    pallas_call x1, Pallas kernels, body(): call(cross_kernel, [(shape(OWN, 16384), WHOLE)], [WHOLE] * 5, [flat], flo...  4.8 us
    pallas_call x1, Pallas kernels, body(): call(filter_kernel, [(shape(SPARE, 128, 256), WHOLE)], [WHOLE] * 5, [flat...  4.43 us
  transfers between devices with their start and end apart: 4, of which 4 were waited for; matrix products, arithmetic and copies ran while one was open for 1% of the time, Pallas kernels for 8%

profile of v3, /device:TPU:24, one launch (start us, length us, event | category | flops | bytes accessed | tf_op | source)
XLA Modules:
  0.0 124.6 jit_solution(2012180741764845253)
XLA Ops:
  0.6 0.0 copy-start.12
  0.6 2.4 %shard_map.189 = bf16[64,16,512]{2,1,0:T(8,128)(2,1)} custom-call(bf16[256,512]{1,0:T(8,128)(2,1)} %q.3, bf16[256,512]{1,0:T(8,128)(2,1)} %k.3, bf16[256,512]{1,0:T(8,128)(2,1)} %v.3, bf16[256,512]{1,0:T(8,128)(2,1)} %c.3), custom_call_target="tpu_custom_call" | custom-call | bytes 2097152 | tf_op jit(solution)/shard_map/pallas_call | solution.py:394
  3.0 0.0 copy-start.9
  3.0 18.6 %all-to-all-start = ((bf16[64,16,512]{2,1,0:T(8,128)(2,1)}), bf16[64,16,512]{2,1,0:T(8,128)(2,1)S(1)}, u32[]{:S(2)}, u32[]{:S(2)}) async-start(bf16[64,16,512]{2,1,0:T(8,128)(2,1)} %shard_map.189), calls=%async_computation | async-start | bytes 2097152 | tf_op jit(solution)/shard_map/all_to_all | solution.py:395
  21.6 0.0 copy-done.12
  21.6 0.1 copy.22.skip
  21.7 0.0 copy-start.11
  21.7 4.4 %shard_map.190.after.filt = f32[24,128,256]{2,1,0:T(8,128)} custom-call(f32[8,16384]{1,0:T(8,128)} %f.1, bf16[256,384]{1,0:T(8,128)(2,1)} %constant.20.clone.first, f32[128,128]{1,0:T(8,128)} %constant.21.clone.tr, f32[128,128]{1,0:T(8,128)} %constant.22.clone.ti, bf16[768,256]{1,0:T(8,128)(2,1)} %constant.23.clone.last), custom_call_target="tpu_custom_call" | custom-call | flops 1000000000 | bytes 2097152 | tf_op jit(solution)/shard_map/pallas_call | solution.py:398
  26.2 0.0 copy-done.9
  26.2 1.9 %copy-done = f32[24,128,256]{2,1,0:T(8,128)S(1)} copy-done((f32[24,128,256]{2,1,0:T(8,128)S(1)}, f32[24,128,256]{2,1,0:T(8,128)}, u32[]{:S(2)}) %copy-start) | copy-done | bytes 3145752
  28.0 0.1 shard_map.191.w
  28.1 0.0 copy-start.3
  28.2 0.0 copy-start.1
  28.2 0.0 copy-start.2
  28.2 0.0 slice-start
  28.2 47.3 %all-to-all-done.x = bf16[64,16,512]{2,1,0:T(8,128)(2,1)S(1)} async-done(((bf16[64,16,512]{2,1,0:T(8,128)(2,1)}), bf16[64,16,512]{2,1,0:T(8,128)(2,1)S(1)}, u32[]{:S(2)}, u32[]{:S(2)}) %all-to-all-start) | async-done | bytes 1048608 | tf_op jit(solution)/shard_map/all_to_all | solution.py:395
  75.4 0.0 copy-done.5
  75.5 0.0 copy-done.6
  75.5 0.0 copy-done.7
  75.5 0.0 copy-done.8
  75.5 7.0 %shard_map.192 = (bf16[64,2,2176]{2,1,0:T(2,128)(2,1)}, f32[24,128,256]{2,1,0:T(8,128)}, f32[8,128]{1,0:T(8,128)S(1)}) custom-call(bf16[64,16,512]{2,1,0:T(8,128)(2,1)S(1)} %all-to-all-done.x, f32[10,8,128]{2,1,0:T(8,128)S(1)} %shard_map.191.w, f32[24,128,256]{2,1,0:T(8,128)} %shard_map.190.after.filt, bf16[256,256]{1,0:T(8,128)(2,1)S(1)} %copy-done.11, ...), custom_call_target="tpu_custom_call" | custom-call | flops 4000000000 | bytes 4194304 | tf_op jit(solution)/shard_map/pallas_call | solution.py:412
  82.5 0.0 copy-start.4
  82.6 6.9 %all-to-all-start.1 = ((bf16[64,2,2176]{2,1,0:T(2,128)(2,1)}), bf16[64,2,2176]{2,1,0:T(2,128)(2,1)S(1)}, u32[]{:S(2)}, u32[]{:S(2)}) async-start(bf16[64,2,2176]{2,1,0:T(2,128)(2,1)} %get-tuple-element.18), calls=%async_computation.1 | async-start | bytes 1114112 | tf_op jit(solution)/shard_map/all_to_all | solution.py:416
  89.6 3.5 %collective-permute-start = (bf16[6,512]{1,0:T(8,128)(2,1)S(1)}, bf16[6,512]{1,0:T(8,128)(2,1)S(1)}, u32[]{:S(2)}, u32[]{:S(2)}) collective-permute-start(bf16[6,512]{1,0:T(8,128)(2,1)S(1)} %pad_maximum_fusion), channel_id=1, source_target_pairs={{0,8},{8,16},{16,24},{24,32},{32,40},{40,48},{48,56},{56,64},{64,7... | collective-permute-start | bytes 18440 | tf_op jit(solution)/shard_map/ppermute | solution.py:409
  93.1 1.3 %collective-permute-start.1 = (bf16[6,512]{1,0:T(8,128)(2,1)S(1)}, bf16[6,512]{1,0:T(8,128)(2,1)S(1)}, u32[]{:S(2)}, u32[]{:S(2)}) collective-permute-start(bf16[6,512]{1,0:T(8,128)(2,1)S(1)} %pad_maximum_fusion.1), channel_id=1, source_target_pairs={{8,0},{16,8},{24,16},{32,24},{40,32},{48,40},{56,48},{64,56},{72,6... | collective-permute-start | bytes 18440 | tf_op jit(solution)/shard_map/ppermute | solution.py:410
  94.4 13.7 %collective-permute-done = bf16[6,512]{1,0:T(8,128)(2,1)S(1)} collective-permute-done((bf16[6,512]{1,0:T(8,128)(2,1)S(1)}, bf16[6,512]{1,0:T(8,128)(2,1)S(1)}, u32[]{:S(2)}, u32[]{:S(2)}) %collective-permute-start) | collective-permute-done | bytes 6176 | tf_op jit(solution)/shard_map/ppermute | solution.py:409
  108.1 5.2 %collective-permute-done.1 = bf16[6,512]{1,0:T(8,128)(2,1)S(1)} collective-permute-done((bf16[6,512]{1,0:T(8,128)(2,1)S(1)}, bf16[6,512]{1,0:T(8,128)(2,1)S(1)}, u32[]{:S(2)}, u32[]{:S(2)}) %collective-permute-start.1) | collective-permute-done | bytes 6176 | tf_op jit(solution)/shard_map/ppermute | solution.py:410
  113.3 0.8 shard_map.193
  114.1 4.8 %shard_map.195 = f32[8,16384]{1,0:T(8,128)} custom-call(f32[24,128,256]{2,1,0:T(8,128)} %get-tuple-element.26.cross, f32[128,128]{1,0:T(8,128)} %constant.21.clone.tr, f32[128,128]{1,0:T(8,128)} %constant.22.clone.ti, bf16[768,256]{1,0:T(8,128)(2,1)} %constant.25.clone.last_back, bf16[128,768]{1,0:T(8,128)(2,1)} %constant.26.clone.first_back), custom_call_target="tpu_custom_call" | custom-call | flops 1000000000 | bytes 2097152 | tf_op jit(solution)/shard_map/pallas_call | solution.py:418
  118.9 0.6 slice_reduce_fusion
  119.5 3.0 %all-to-all-done.1.got = bf16[64,2,2176]{2,1,0:T(2,128)(2,1)S(1)} async-done(((bf16[64,2,2176]{2,1,0:T(2,128)(2,1)}), bf16[64,2,2176]{2,1,0:T(2,128)(2,1)S(1)}, u32[]{:S(2)}, u32[]{:S(2)}) %all-to-all-start.1) | async-done | bytes 557088 | tf_op jit(solution)/shard_map/all_to_all | solution.py:416
  122.5 2.1 %shard_map.194 = (bf16[256,512]{1,0:T(8,128)(2,1)}, bf16[256,512]{1,0:T(8,128)(2,1)}, bf16[256,512]{1,0:T(8,128)(2,1)}, bf16[256,512]{1,0:T(8,128)(2,1)}, f32[3,3,512]{2,1,0:T(4,128)}) custom-call(bf16[64,2,2176]{2,1,0:T(2,128)(2,1)S(1)} %all-to-all-done.1.got, bf16[256,512]{1,0:T(8,128)(2,1)S(1)} %get-tuple-element.19.query, ...), custom_call_target="tpu_custom_call" | custom-call | bytes 3145728 | tf_op jit(solution)/shard_map/pallas_call | solution.py:426
  (19 shorter events, 0.1 us)
Async XLA Ops:
  0.6 21.0 %copy-start.12 = (f32[8]{0:T(128)S(1)}, f32[8]{0:T(128)}, u32[]{:S(2)}) copy-start(f32[8]{0:T(128)} %param.19) | copy-start | bytes 100
  3.0 23.1 %copy-start.9 = (f32[3,3,512]{2,1,0:T(4,128)S(1)}, f32[3,3,512]{2,1,0:T(4,128)}, u32[]{:S(2)}) copy-start(f32[3,3,512]{2,1,0:T(4,128)} %w.5) | copy-start | bytes 55300
  3.0 72.4 %all-to-all-start = ((bf16[64,16,512]{2,1,0:T(8,128)(2,1)}), bf16[64,16,512]{2,1,0:T(8,128)(2,1)S(1)}, u32[]{:S(2)}, u32[]{:S(2)}) async-start(bf16[64,16,512]{2,1,0:T(8,128)(2,1)} %shard_map.189), calls=%async_computation | async-start | bytes 2097152 | tf_op jit(solution)/shard_map/all_to_all | solution.py:395
  21.7 53.8 %copy-start.5 = (bf16[768,256]{1,0:T(8,128)(2,1)S(1)}, bf16[768,256]{1,0:T(8,128)(2,1)}, u32[]{:S(2)}) copy-start(bf16[768,256]{1,0:T(8,128)(2,1)} %constant.25.clone.last_back) | copy-start | bytes 1179652
  21.7 53.8 %copy-start.6 = (bf16[768,256]{1,0:T(8,128)(2,1)S(1)}, bf16[768,256]{1,0:T(8,128)(2,1)}, u32[]{:S(2)}) copy-start(bf16[768,256]{1,0:T(8,128)(2,1)} %constant.23.clone.last) | copy-start | bytes 1179652
  21.7 53.8 %copy-start.7 = (f32[128,128]{1,0:T(8,128)S(1)}, f32[128,128]{1,0:T(8,128)}, u32[]{:S(2)}) copy-start(f32[128,128]{1,0:T(8,128)} %constant.21.clone.tr) | copy-start | bytes 196612
  21.7 53.8 %copy-start.8 = (f32[128,128]{1,0:T(8,128)S(1)}, f32[128,128]{1,0:T(8,128)}, u32[]{:S(2)}) copy-start(f32[128,128]{1,0:T(8,128)} %constant.22.clone.ti) | copy-start | bytes 196612
  21.7 53.8 %copy-start.10 = (bf16[128,768]{1,0:T(8,128)(2,1)S(1)}, bf16[128,768]{1,0:T(8,128)(2,1)}, u32[]{:S(2)}) copy-start(bf16[128,768]{1,0:T(8,128)(2,1)} %constant.26.clone.first_back) | copy-start | bytes 589828
  21.7 53.8 %copy-start.11 = (bf16[256,256]{1,0:T(8,128)(2,1)S(1)}, bf16[256,256]{1,0:T(8,128)(2,1)}, u32[]{:S(2)}) copy-start(bf16[256,256]{1,0:T(8,128)(2,1)} %constant.24.clone.first) | copy-start | bytes 393220
  26.2 1.9 %copy-start = (f32[24,128,256]{2,1,0:T(8,128)S(1)}, f32[24,128,256]{2,1,0:T(8,128)}, u32[]{:S(2)}) copy-start(f32[24,128,256]{2,1,0:T(8,128)} %shard_map.190.after.filt) | copy-start | bytes 9437188
  28.1 61.4 %copy-start.3 = (bf16[256,512]{1,0:T(8,128)(2,1)S(1)}, bf16[256,512]{1,0:T(8,128)(2,1)}, u32[]{:S(2)}) copy-start(bf16[256,512]{1,0:T(8,128)(2,1)} %q.3) | copy-start | bytes 786436
  28.2 61.4 %copy-start.1 = (bf16[256,512]{1,0:T(8,128)(2,1)S(1)}, bf16[256,512]{1,0:T(8,128)(2,1)}, u32[]{:S(2)}) copy-start(bf16[256,512]{1,0:T(8,128)(2,1)} %k.3) | copy-start | bytes 786436
  28.2 61.4 %copy-start.2 = (bf16[256,512]{1,0:T(8,128)(2,1)S(1)}, bf16[256,512]{1,0:T(8,128)(2,1)}, u32[]{:S(2)}) copy-start(bf16[256,512]{1,0:T(8,128)(2,1)} %v.3) | copy-start | bytes 786436
  28.2 64.9 %slice-start = ((bf16[256,512]{1,0:T(8,128)(2,1)}), bf16[2,512]{1,0:T(2,128)(2,1)S(1)}, s32[]{:S(2)}) async-start(bf16[256,512]{1,0:T(8,128)(2,1)} %c.3), calls=%async_computation.2 | async-start | bytes 4096 | tf_op jit(solution)/shard_map/slice | solution.py:408
  82.5 40.0 %copy-start.4 = (bf16[256,512]{1,0:T(8,128)(2,1)S(1)}, bf16[256,512]{1,0:T(8,128)(2,1)}, u32[]{:S(2)}) copy-start(bf16[256,512]{1,0:T(8,128)(2,1)} %c.3) | copy-start | bytes 786436
  82.6 39.9 %all-to-all-start.1 = ((bf16[64,2,2176]{2,1,0:T(2,128)(2,1)}), bf16[64,2,2176]{2,1,0:T(2,128)(2,1)S(1)}, u32[]{:S(2)}, u32[]{:S(2)}) async-start(bf16[64,2,2176]{2,1,0:T(2,128)(2,1)} %get-tuple-element.18), calls=%async_computation.1 | async-start | bytes 1114112 | tf_op jit(solution)/shard_map/all_to_all | solution.py:416
  89.6 18.5 %collective-permute-start = (bf16[6,512]{1,0:T(8,128)(2,1)S(1)}, bf16[6,512]{1,0:T(8,128)(2,1)S(1)}, u32[]{:S(2)}, u32[]{:S(2)}) collective-permute-start(bf16[6,512]{1,0:T(8,128)(2,1)S(1)} %pad_maximum_fusion), channel_id=1, source_target_pairs={{0,8},{8,16},{16,24},{24,32},{32,40},{40,48},{48,56},{56,64},{64,7... | collective-permute-start | bytes 18440 | tf_op jit(solution)/shard_map/ppermute | solution.py:409
  93.1 20.2 %collective-permute-start.1 = (bf16[6,512]{1,0:T(8,128)(2,1)S(1)}, bf16[6,512]{1,0:T(8,128)(2,1)S(1)}, u32[]{:S(2)}, u32[]{:S(2)}) collective-permute-start(bf16[6,512]{1,0:T(8,128)(2,1)S(1)} %pad_maximum_fusion.1), channel_id=1, source_target_pairs={{8,0},{16,8},{24,16},{32,24},{40,32},{48,40},{56,48},{64,56},{72,6... | collective-permute-start | bytes 18440 | tf_op jit(solution)/shard_map/ppermute | solution.py:410

commit v4 on v3

--- a/solution.py
+++ b/solution.py
@@ -404,11 +404,6 @@
         [pl.BlockSpec(memory_space=pltpu.SMEM), WHOLE, WHOLE, HBM], moved=1 << 20,
     )(here, short_weights, skip_gain[:, None], spectrum)
 
-    ends = jnp.concatenate([query_in[254:], key_in[254:], value_in[254:]], axis=0)
-    starts = jnp.concatenate([key_in[:2], value_in[:2], cotangent[:2]], axis=0)
-    prev = lax.ppermute(ends, "ctx", [(i, i + 1) for i in range(count - 1)]).astype(F32)
-    nxt = lax.ppermute(starts, "ctx", [(i + 1, i) for i in range(count - 1)]).astype(F32)
-
     answer, cross, dskip = channels()(
         seqs, own_w, spectrum, t["first_pair"], *turns, t["last"], t["last_back"], t["first_back"]
     )
@@ -418,6 +413,12 @@
     d_filter = call(
         cross_kernel, [(shape(OWN, 16384), WHOLE)], [WHOLE] * 5, [flat], flops=10**9, moved=2 << 20, limit=60
     )(cross, *turns, t["last_back"], t["first_back"])
+
+    ends = jnp.concatenate([query_in[254:], key_in[254:], value_in[254:]], axis=0)
+    starts = jnp.concatenate([key_in[:2], value_in[:2], cotangent[:2]], axis=0)
+    ends, starts, _ = lax.optimization_barrier((ends, starts, d_filter))
+    prev = lax.ppermute(ends, "ctx", [(i, i + 1) for i in range(count - 1)]).astype(F32)
+    nxt = lax.ppermute(starts, "ctx", [(i + 1, i) for i in range(count - 1)]).astype(F32)
 
     extended = shape(264, 512)
     query, conv_k, conv_v = call(

time: 125 us -> 125 us (level)
    ppermute x1, waiting for transfers between devices: 13.7 us -> 0.01 us  [body(): lax.ppermute(ends, 'ctx', [(i, i + 1) for i in range(count - 1)])]
    ppermute x1, waiting for transfers between devices: 5.24 us -> 12.4 us  [body(): lax.ppermute(starts, 'ctx', [(i + 1, i) for i in range(count - 1)])]
    all_to_all x1, waiting for transfers between devices: 2.98 us -> 8.4 us  [body(): got = lax.all_to_all(answer, 'ctx', split_axis=0, concat_axis=0, tiled=True)]
  transfers between devices with their start and end apart: 4 -> 4, of which waited for: 4 -> 3; matrix products, arithmetic and copies ran while one was open for 1% -> 1% of each run, Pallas kernels for 8% -> 8%
where the time goes in v4:
time: 125 us
  waiting for transfers between devices  68.1 us (54%)
  starting transfers between devices  31.3 us (25%)
  Pallas kernels  21.5 us (17%)
  local copies, waits for them, and re-layouts  2.7 us (2%)
    all_to_all x1, waiting for transfers between devices, body(): lax.all_to_all(packed, 'ctx', split_axis=0, concat_axis=0, tiled=True)  47.3 us
    all_to_all x1, starting transfers between devices, body(): lax.all_to_all(packed, 'ctx', split_axis=0, concat_axis=0, tiled=True)  18.6 us
    ppermute x1, waiting for transfers between devices, body(): lax.ppermute(starts, 'ctx', [(i + 1, i) for i in range(count - 1)])  12.4 us
    all_to_all x1, waiting for transfers between devices, body(): got = lax.all_to_all(answer, 'ctx', split_axis=0, concat_axis=0, tiled=True)  8.4 us
    pallas_call x1, Pallas kernels, body(): channels()  6.99 us
    all_to_all x1, starting transfers between devices, body(): got = lax.all_to_all(answer, 'ctx', split_axis=0, concat_axis=0, tiled=True)  6.92 us
    pallas_call x1, Pallas kernels, body(): call(cross_kernel, [(shape(OWN, 16384), WHOLE)], [WHOLE] * 5, [flat], flo...  4.8 us
    ppermute x1, starting transfers between devices, body(): lax.ppermute(ends, 'ctx', [(i, i + 1) for i in range(count - 1)])  4.55 us
  transfers between devices with their start and end apart: 4, of which 3 were waited for; matrix products, arithmetic and copies ran while one was open for 1% of the time, Pallas kernels for 8%

profile of v4, /device:TPU:24, one launch (start us, length us, event | category | flops | bytes accessed | tf_op | source)
XLA Modules:
  0.0 124.5 jit_solution(16391502078674657680)
XLA Ops:
  0.6 0.0 copy-start.12
  0.6 2.4 %shard_map.189 = bf16[64,16,512]{2,1,0:T(8,128)(2,1)} custom-call(bf16[256,512]{1,0:T(8,128)(2,1)} %q.3, bf16[256,512]{1,0:T(8,128)(2,1)} %k.3, bf16[256,512]{1,0:T(8,128)(2,1)} %v.3, bf16[256,512]{1,0:T(8,128)(2,1)} %c.3), custom_call_target="tpu_custom_call" | custom-call | bytes 2097152 | tf_op jit(solution)/shard_map/pallas_call | solution.py:394
  3.0 0.0 copy-start.9
  3.0 18.6 %all-to-all-start = ((bf16[64,16,512]{2,1,0:T(8,128)(2,1)}), bf16[64,16,512]{2,1,0:T(8,128)(2,1)S(1)}, u32[]{:S(2)}, u32[]{:S(2)}) async-start(bf16[64,16,512]{2,1,0:T(8,128)(2,1)} %shard_map.189), calls=%async_computation | async-start | bytes 2097152 | tf_op jit(solution)/shard_map/all_to_all | solution.py:395
  21.6 0.0 copy-done.12
  21.6 0.1 copy.22.skip
  21.7 0.0 copy-start.11
  21.7 4.4 %shard_map.190.after.filt = f32[24,128,256]{2,1,0:T(8,128)} custom-call(f32[8,16384]{1,0:T(8,128)} %f.1, bf16[256,384]{1,0:T(8,128)(2,1)} %constant.20.clone.first, f32[128,128]{1,0:T(8,128)} %constant.21.clone.tr, f32[128,128]{1,0:T(8,128)} %constant.22.clone.ti, bf16[768,256]{1,0:T(8,128)(2,1)} %constant.23.clone.last), custom_call_target="tpu_custom_call" | custom-call | flops 1000000000 | bytes 2097152 | tf_op jit(solution)/shard_map/pallas_call | solution.py:398
  26.1 0.0 copy-done.9
  26.1 1.9 %copy-done = f32[24,128,256]{2,1,0:T(8,128)S(1)} copy-done((f32[24,128,256]{2,1,0:T(8,128)S(1)}, f32[24,128,256]{2,1,0:T(8,128)}, u32[]{:S(2)}) %copy-start) | copy-done | bytes 3145752
  28.0 0.1 shard_map.191.w
  28.1 0.0 copy-start.3
  28.1 0.0 copy-start.1
  28.2 0.0 copy-start.2
  28.2 0.0 slice-start
  28.2 47.3 %all-to-all-done.x = bf16[64,16,512]{2,1,0:T(8,128)(2,1)S(1)} async-done(((bf16[64,16,512]{2,1,0:T(8,128)(2,1)}), bf16[64,16,512]{2,1,0:T(8,128)(2,1)S(1)}, u32[]{:S(2)}, u32[]{:S(2)}) %all-to-all-start) | async-done | bytes 1048608 | tf_op jit(solution)/shard_map/all_to_all | solution.py:395
  75.4 0.0 copy-done.5
  75.5 0.0 copy-done.8
  75.5 0.0 copy-done.10
  75.5 0.0 copy-done.11
  75.5 7.0 %shard_map.192 = (bf16[64,2,2176]{2,1,0:T(2,128)(2,1)}, f32[24,128,256]{2,1,0:T(8,128)}, f32[8,128]{1,0:T(8,128)S(1)}) custom-call(bf16[64,16,512]{2,1,0:T(8,128)(2,1)S(1)} %all-to-all-done.x, f32[10,8,128]{2,1,0:T(8,128)S(1)} %shard_map.191.w, f32[24,128,256]{2,1,0:T(8,128)} %shard_map.190.after.filt, bf16[256,256]{1,0:T(8,128)(2,1)S(1)} %copy-done.11, ...), custom_call_target="tpu_custom_call" | custom-call | flops 4000000000 | bytes 4194304 | tf_op jit(solution)/shard_map/pallas_call | solution.py:407
  82.5 0.0 copy-start.4
  82.5 6.9 %all-to-all-start.1 = ((bf16[64,2,2176]{2,1,0:T(2,128)(2,1)}), bf16[64,2,2176]{2,1,0:T(2,128)(2,1)S(1)}, u32[]{:S(2)}, u32[]{:S(2)}) async-start(bf16[64,2,2176]{2,1,0:T(2,128)(2,1)} %get-tuple-element.20), calls=%async_computation.1 | async-start | bytes 1114112 | tf_op jit(solution)/shard_map/all_to_all | solution.py:411
  89.5 4.8 %shard_map.193 = f32[8,16384]{1,0:T(8,128)} custom-call(f32[24,128,256]{2,1,0:T(8,128)} %get-tuple-element.21.cross, f32[128,128]{1,0:T(8,128)} %constant.21.clone.tr, f32[128,128]{1,0:T(8,128)} %constant.22.clone.ti, bf16[768,256]{1,0:T(8,128)(2,1)} %constant.25.clone.last_back, bf16[128,768]{1,0:T(8,128)(2,1)} %constant.26.clone.first_back), custom_call_target="tpu_custom_call" | custom-call | flops 1000000000 | bytes 2097152 | tf_op jit(solution)/shard_map/pallas_call | solution.py:413
  94.3 1.3 %collective-permute-start.1 = (bf16[6,512]{1,0:T(8,128)(2,1)S(1)}, bf16[6,512]{1,0:T(8,128)(2,1)S(1)}, u32[]{:S(2)}, u32[]{:S(2)}) collective-permute-start(bf16[6,512]{1,0:T(8,128)(2,1)S(1)} %get-tuple-element.23), channel_id=1, source_target_pairs={{8,0},{16,8},{24,16},{32,24},{40,32},{48,40},{56,48},{64,56},{72,6... | collective-permute-start | bytes 18440 | tf_op jit(solution)/shard_map/ppermute | solution.py:421
  95.6 4.5 %collective-permute-start = (bf16[6,512]{1,0:T(8,128)(2,1)S(1)}, bf16[6,512]{1,0:T(8,128)(2,1)S(1)}, u32[]{:S(2)}, u32[]{:S(2)}) collective-permute-start(bf16[6,512]{1,0:T(8,128)(2,1)S(1)} %get-tuple-element.22), channel_id=1, source_target_pairs={{0,8},{8,16},{16,24},{24,32},{32,40},{40,48},{48,56},{56,64},{64,7... | collective-permute-start | bytes 18440 | tf_op jit(solution)/shard_map/ppermute | solution.py:420
  100.2 0.6 slice_reduce_fusion
  100.8 12.4 %collective-permute-done.1 = bf16[6,512]{1,0:T(8,128)(2,1)S(1)} collective-permute-done((bf16[6,512]{1,0:T(8,128)(2,1)S(1)}, bf16[6,512]{1,0:T(8,128)(2,1)S(1)}, u32[]{:S(2)}, u32[]{:S(2)}) %collective-permute-start.1) | collective-permute-done | bytes 6176 | tf_op jit(solution)/shard_map/ppermute | solution.py:421
  113.2 0.0 collective-permute-done
  113.2 0.8 shard_map.194
  114.0 8.4 %all-to-all-done.1.got = bf16[64,2,2176]{2,1,0:T(2,128)(2,1)S(1)} async-done(((bf16[64,2,2176]{2,1,0:T(2,128)(2,1)}), bf16[64,2,2176]{2,1,0:T(2,128)(2,1)S(1)}, u32[]{:S(2)}, u32[]{:S(2)}) %all-to-all-start.1) | async-done | bytes 557088 | tf_op jit(solution)/shard_map/all_to_all | solution.py:411
  122.4 2.1 %shard_map.195 = (bf16[256,512]{1,0:T(8,128)(2,1)}, bf16[256,512]{1,0:T(8,128)(2,1)}, bf16[256,512]{1,0:T(8,128)(2,1)}, bf16[256,512]{1,0:T(8,128)(2,1)}, f32[3,3,512]{2,1,0:T(4,128)}) custom-call(bf16[64,2,2176]{2,1,0:T(2,128)(2,1)S(1)} %all-to-all-done.1.got, bf16[256,512]{1,0:T(8,128)(2,1)S(1)} %get-tuple-element.24.query, ...), custom_call_target="tpu_custom_call" | custom-call | bytes 3145728 | tf_op jit(solution)/shard_map/pallas_call | solution.py:427
  (19 shorter events, 0.1 us)
Async XLA Ops:
  0.6 21.0 %copy-start.12 = (f32[8]{0:T(128)S(1)}, f32[8]{0:T(128)}, u32[]{:S(2)}) copy-start(f32[8]{0:T(128)} %param.19) | copy-start | bytes 100
  3.0 23.1 %copy-start.9 = (f32[3,3,512]{2,1,0:T(4,128)S(1)}, f32[3,3,512]{2,1,0:T(4,128)}, u32[]{:S(2)}) copy-start(f32[3,3,512]{2,1,0:T(4,128)} %w.5) | copy-start | bytes 55300
  3.0 72.4 %all-to-all-start = ((bf16[64,16,512]{2,1,0:T(8,128)(2,1)}), bf16[64,16,512]{2,1,0:T(8,128)(2,1)S(1)}, u32[]{:S(2)}, u32[]{:S(2)}) async-start(bf16[64,16,512]{2,1,0:T(8,128)(2,1)} %shard_map.189), calls=%async_computation | async-start | bytes 2097152 | tf_op jit(solution)/shard_map/all_to_all | solution.py:395
  21.7 53.8 %copy-start.5 = (bf16[768,256]{1,0:T(8,128)(2,1)S(1)}, bf16[768,256]{1,0:T(8,128)(2,1)}, u32[]{:S(2)}) copy-start(bf16[768,256]{1,0:T(8,128)(2,1)} %constant.25.clone.last_back) | copy-start | bytes 1179652
  21.7 53.8 %copy-start.6 = (bf16[768,256]{1,0:T(8,128)(2,1)S(1)}, bf16[768,256]{1,0:T(8,128)(2,1)}, u32[]{:S(2)}) copy-start(bf16[768,256]{1,0:T(8,128)(2,1)} %constant.23.clone.last) | copy-start | bytes 1179652
  21.7 53.8 %copy-start.7 = (f32[128,128]{1,0:T(8,128)S(1)}, f32[128,128]{1,0:T(8,128)}, u32[]{:S(2)}) copy-start(f32[128,128]{1,0:T(8,128)} %constant.21.clone.tr) | copy-start | bytes 196612
  21.7 53.8 %copy-start.8 = (f32[128,128]{1,0:T(8,128)S(1)}, f32[128,128]{1,0:T(8,128)}, u32[]{:S(2)}) copy-start(f32[128,128]{1,0:T(8,128)} %constant.22.clone.ti) | copy-start | bytes 196612
  21.7 53.8 %copy-start.10 = (bf16[128,768]{1,0:T(8,128)(2,1)S(1)}, bf16[128,768]{1,0:T(8,128)(2,1)}, u32[]{:S(2)}) copy-start(bf16[128,768]{1,0:T(8,128)(2,1)} %constant.26.clone.first_back) | copy-start | bytes 589828
  21.7 53.8 %copy-start.11 = (bf16[256,256]{1,0:T(8,128)(2,1)S(1)}, bf16[256,256]{1,0:T(8,128)(2,1)}, u32[]{:S(2)}) copy-start(bf16[256,256]{1,0:T(8,128)(2,1)} %constant.24.clone.first) | copy-start | bytes 393220
  26.1 1.9 %copy-start = (f32[24,128,256]{2,1,0:T(8,128)S(1)}, f32[24,128,256]{2,1,0:T(8,128)}, u32[]{:S(2)}) copy-start(f32[24,128,256]{2,1,0:T(8,128)} %shard_map.190.after.filt) | copy-start | bytes 9437188
  28.1 61.3 %copy-start.3 = (bf16[256,512]{1,0:T(8,128)(2,1)S(1)}, bf16[256,512]{1,0:T(8,128)(2,1)}, u32[]{:S(2)}) copy-start(bf16[256,512]{1,0:T(8,128)(2,1)} %q.3) | copy-start | bytes 786436
  28.1 61.3 %copy-start.1 = (bf16[256,512]{1,0:T(8,128)(2,1)S(1)}, bf16[256,512]{1,0:T(8,128)(2,1)}, u32[]{:S(2)}) copy-start(bf16[256,512]{1,0:T(8,128)(2,1)} %k.3) | copy-start | bytes 786436
  28.2 61.3 %copy-start.2 = (bf16[256,512]{1,0:T(8,128)(2,1)S(1)}, bf16[256,512]{1,0:T(8,128)(2,1)}, u32[]{:S(2)}) copy-start(bf16[256,512]{1,0:T(8,128)(2,1)} %v.3) | copy-start | bytes 786436
  28.2 61.3 %slice-start = ((bf16[256,512]{1,0:T(8,128)(2,1)}), bf16[2,512]{1,0:T(2,128)(2,1)S(1)}, s32[]{:S(2)}) async-start(bf16[256,512]{1,0:T(8,128)(2,1)} %c.3), calls=%async_computation.2 | async-start | bytes 4096 | tf_op jit(solution)/shard_map/slice | solution.py:418
  82.5 39.9 %copy-start.4 = (bf16[256,512]{1,0:T(8,128)(2,1)S(1)}, bf16[256,512]{1,0:T(8,128)(2,1)}, u32[]{:S(2)}) copy-start(bf16[256,512]{1,0:T(8,128)(2,1)} %c.3) | copy-start | bytes 786436
  82.5 39.9 %all-to-all-start.1 = ((bf16[64,2,2176]{2,1,0:T(2,128)(2,1)}), bf16[64,2,2176]{2,1,0:T(2,128)(2,1)S(1)}, u32[]{:S(2)}, u32[]{:S(2)}) async-start(bf16[64,2,2176]{2,1,0:T(2,128)(2,1)} %get-tuple-element.20), calls=%async_computation.1 | async-start | bytes 1114112 | tf_op jit(solution)/shard_map/all_to_all | solution.py:411
  94.3 18.9 %collective-permute-start.1 = (bf16[6,512]{1,0:T(8,128)(2,1)S(1)}, bf16[6,512]{1,0:T(8,128)(2,1)S(1)}, u32[]{:S(2)}, u32[]{:S(2)}) collective-permute-start(bf16[6,512]{1,0:T(8,128)(2,1)S(1)} %get-tuple-element.23), channel_id=1, source_target_pairs={{8,0},{16,8},{24,16},{32,24},{40,32},{48,40},{56,48},{64,56},{72,6... | collective-permute-start | bytes 18440 | tf_op jit(solution)/shard_map/ppermute | solution.py:421
  95.6 17.6 %collective-permute-start = (bf16[6,512]{1,0:T(8,128)(2,1)S(1)}, bf16[6,512]{1,0:T(8,128)(2,1)S(1)}, u32[]{:S(2)}, u32[]{:S(2)}) collective-permute-start(bf16[6,512]{1,0:T(8,128)(2,1)S(1)} %get-tuple-element.22), channel_id=1, source_target_pairs={{0,8},{8,16},{16,24},{24,32},{32,40},{40,48},{48,56},{56,64},{64,7... | collective-permute-start | bytes 18440 | tf_op jit(solution)/shard_map/ppermute | solution.py:420
